TPU v7x, 32 devices: a whole 2x2x4 slice. The times are simulated.
32 devices in a mesh: seq: 4 (over x, core), tp: 8 (over z, y).
Axes of the slice: x: 2, y: 2, z: 4, core: 2. Of those that a mesh axis runs over, the one named last changes fastest.
Arguments:
- clean_in: bfloat16 [4, 1024, 5120], P(None, 'seq', 'tp'), may hold values from -6 to 6
- noise_mask: int32 [4, 1024], P(None, 'seq'), may hold values from 0 to 1
- mask_embed: bfloat16 [5120], P('tp'), may hold values from -6 to 6
- norm_gain: float32 [5120], replicated, may hold values from 0.1 to 1.9
- q_weight: bfloat16 [5120, 4096], P(None, 'tp'), may hold values from -0.078125 to 0.078125
- q_bias: float32 [4096], P('tp'), may hold values from -60 to 60
- k_weight: bfloat16 [5120, 1024], replicated, may hold values from -0.078125 to 0.078125
- v_weight: bfloat16 [5120, 1024], replicated, may hold values from -0.078125 to 0.078125
- v_bias: float32 [1024], replicated, may hold values from -3 to 3
- o_weight: bfloat16 [4096, 5120], P('tp'), may hold values from -0.125 to 0.125
Outputs:
- clean_out: bfloat16 [4, 1024, 5120], P(None, 'seq', 'tp')
- noisy_out: bfloat16 [4, 1024, 5120], P(None, 'seq', 'tp')
All inputs are finite; a program needn't handle non-finite values.
Results may differ from a plain program's by a relative error of at most 0.013.
The roundings to bfloat16 on the way count: a program that leaves them out, or rounds other values in their place, can miss the bound.
Values may be sent and summed in bfloat16 or wider, within the bound.
A program may use at most 192 MiB of HBM per device.

v0:
```python
import math

import jax
import jax.numpy as jnp
from jax import lax
from jax.sharding import PartitionSpec as P

HD = 128
KVH = 8
BLOCK = 32


eps = 1e-06
theta = 1000000.0


def from_behind(block, axis, distance):
    devices = range(lax.axis_size(axis))
    route = [(i - distance, i) for i in devices if i - distance in devices]
    return lax.ppermute(block, axis, route)


def rotate(values, positions):
    half = values.shape[-1] // 2
    freqs = theta ** (-(jnp.arange(half).astype(jnp.float32) * 2.0) / values.shape[-1])
    angles = positions[:, None] * freqs[None, :]
    cosine = jnp.cos(angles)[:, None, :]
    sine = jnp.sin(angles)[:, None, :]
    first = values[..., :half]
    second = values[..., half:]
    return jnp.concatenate(
        [first * cosine - second * sine, second * cosine + first * sine], axis=-1
    )


def update(state, queries, key_rows, value_rows, allowed):
    best, denom, weighted = state
    scores = jnp.einsum("schd,skd->shck", queries, key_rows, preferred_element_type=jnp.float32) * (
        1.0 / math.sqrt(HD)
    )
    scores = jnp.where(allowed[None, None], scores, -1e30)
    new_best = jnp.maximum(best, jnp.max(scores, axis=-1))
    factor = jnp.exp(best - new_best)
    expo = jnp.where(allowed[None, None], jnp.exp(scores - new_best[..., None]), 0.0)
    denom = denom * factor + jnp.sum(expo, axis=-1)
    weighted = weighted * jnp.transpose(factor, (0, 2, 1))[..., None] + jnp.einsum(
        "shck,skd->schd", expo.astype(jnp.bfloat16), value_rows, preferred_element_type=jnp.float32
    )
    return (new_best, denom, weighted)


def per_device(
    clean_in,
    noise_mask,
    mask_embed,
    norm_gain,
    q_weight,
    q_bias,
    k_weight,
    v_weight,
    v_bias,
    o_weight,
):
    doc_count, tokens_dev, local_width = clean_in.shape
    tp_count = lax.axis_size("tp")
    seq_count = lax.axis_size("seq")
    width = local_width * tp_count
    q_cols = q_weight.shape[1]
    heads = q_cols // HD
    my_seq = lax.axis_index("seq")
    my_tp = lax.axis_index("tp")
    head_start = my_tp * KVH // tp_count * HD
    key_cols = lax.dynamic_slice_in_dim(k_weight, head_start, HD, 1)
    value_cols = lax.dynamic_slice_in_dim(v_weight, head_start, HD, 1)
    value_shift = lax.dynamic_slice_in_dim(v_bias, head_start, HD, 0)
    noisy_in = jnp.where(noise_mask[..., None] == 1, mask_embed[None, None, :], clean_in)
    streams = jnp.stack([clean_in, noisy_in])
    whole = lax.all_gather(streams, "tp", axis=3, tiled=True)
    floats = whole.astype(jnp.float32)
    mean_sq = jnp.mean(floats * floats, axis=-1, keepdims=True)
    normed = (floats * lax.rsqrt(mean_sq + eps) * norm_gain).astype(jnp.bfloat16)
    flat_rows = normed.reshape(-1, width)
    queries = jnp.dot(flat_rows, q_weight, preferred_element_type=jnp.float32)
    key_rows = jnp.dot(flat_rows, key_cols, preferred_element_type=jnp.float32)
    value_rows = jnp.dot(flat_rows, value_cols, preferred_element_type=jnp.float32)
    queries = queries + q_bias
    value_rows = value_rows + value_shift
    query_pos = my_seq * tokens_dev + jnp.arange(tokens_dev)
    positions = query_pos.astype(jnp.float32)
    query_block = query_pos // BLOCK
    queries = rotate(queries.reshape(2, doc_count, tokens_dev, heads, HD), positions).astype(
        jnp.bfloat16
    )
    key_rows = rotate(key_rows.reshape(2, doc_count, tokens_dev, 1, HD), positions)[
        ..., 0, :
    ].astype(jnp.bfloat16)
    value_rows = value_rows.reshape(2, doc_count, tokens_dev, HD).astype(jnp.bfloat16)
    clean_pair = jnp.stack([key_rows[0], value_rows[0]])

    def clean_piece(states, piece, start):
        key_pos = start + jnp.arange(piece.shape[2])
        key_block = key_pos // BLOCK
        valid = (key_pos >= 0)[None, :]
        clean_seen = (key_block[None, :] <= query_block[:, None]) & valid
        noisy_seen = (key_block[None, :] < query_block[:, None]) & valid
        return (
            update(states[0], queries[0], piece[0], piece[1], clean_seen),
            update(states[1], queries[1], piece[0], piece[1], noisy_seen),
        )

    empty = (
        jnp.full((doc_count, heads, tokens_dev), -1e30, jnp.float32),
        jnp.zeros((doc_count, heads, tokens_dev), jnp.float32),
        jnp.zeros((doc_count, tokens_dev, heads, HD), jnp.float32),
    )
    states = clean_piece((empty, empty), clean_pair, my_seq * tokens_dev)
    moving = clean_pair
    for hop_count in range(1, seq_count):
        moving = from_behind(moving, "seq", 1)
        states = clean_piece(states, moving, (my_seq - hop_count) * tokens_dev)
    own_block = query_block[None, :] == query_block[:, None]
    noisy_state = update(states[1], queries[1], key_rows[1], value_rows[1], own_block)
    clean_state = states[0]
    finished = []
    for state in (clean_state, noisy_state):
        finished.append(state[2] / jnp.transpose(state[1], (0, 2, 1))[..., None])
    attended = jnp.stack(finished).astype(jnp.bfloat16).reshape(2, doc_count, tokens_dev, q_cols)
    partial_sums = jnp.dot(
        attended.reshape(-1, q_cols), o_weight, preferred_element_type=jnp.float32
    ).reshape(2, doc_count, tokens_dev, width)
    mixed = lax.psum_scatter(
        partial_sums.astype(jnp.bfloat16), "tp", scatter_dimension=3, tiled=True
    ).astype(jnp.float32)
    outputs = (streams.astype(jnp.float32) + mixed).astype(jnp.bfloat16)
    return (outputs[0], outputs[1])


def solution(mesh):
    return jax.shard_map(
        per_device,
        mesh=mesh,
        in_specs=(
            P(None, "seq", "tp"),
            P(None, "seq"),
            P("tp"),
            P(),
            P(None, "tp"),
            P("tp"),
            P(),
            P(),
            P(),
            P("tp", None),
        ),
        out_specs=(P(None, "seq", "tp"), P(None, "seq", "tp")),
        check_vma=False,
    )
```

profile of v0, /device:TPU:0, one launch (start us, length us, event | category | flops | bytes accessed | tf_op | source)
XLA Modules:
  0.0 1006.3 jit_solution(1944741057652172014)
XLA Ops:
  10.5 3.1 pad_maximum_fusion
  15.8 402.6 %all-gather.2.cloned.1.call-done = bf16[2,4,256,5120]{3,2,1,0:T(8,128)(2,1)} async-done(((bf16[2,4,256,640]{3,2,1,0:T(8,128)(2,1)}), bf16[2,4,256,5120]{3,2,1,0:T(8,128)(2,1)}) %all-gather.2.cloned.1.call-update) | async-done | bytes 20971536 | tf_op jit(solution)/shard_map/all_gather | solution.py:78
  418.3 8.8 fusion
  427.2 12.0 %fusion.2 = bf16[2,4,256,5120]{3,2,1,0:T(8,128)(2,1)S(1)} fusion(bf16[2,4,256,5120]{3,2,1,0:T(8,128)(2,1)} %all-gather.2.cloned.1.call-done, f32[5120]{0:T(1024)S(1)} %copy-done.12, f32[2,4,256]{2,1,0:T(4,128)S(1)} %add_rsqrt_fusion), kind=kLoop, calls=%fused_computation.4 | loop fusion | flops 41943040 | bytes 41971712 | tf_op jit(solution)/shard_map/convert_element_type | solution.py:81
  439.2 8.2 fusion.31
  448.1 16.0 %convolution_add_fusion = f32[2048,512]{1,0:T(8,128)} fusion(bf16[2048,5120]{1,0:T(8,128)(2,1)S(1)} %bitcast.461, bf16[5120,512]{1,0:T(8,128)(2,1)} %param.14, f32[512]{0:T(512)S(1)} %copy-done.13), kind=kOutput, calls=%fused_computation.37 | convolution fusion | flops 10738466816 | bytes 30410752 | tf_op jit(solution)/shard_map/dot_general | solution.py:83
  464.1 5.2 reshape.638
  469.3 9.0 fusion.196
  478.4 11.6 %convolution_bitcast_fusion = f32[2,4,256,1,128]{2,4,1,0,3:T(8,128)S(1)} fusion(bf16[2,4,256,5120]{3,2,1,0:T(8,128)(2,1)} %copy-done, bf16[5120,1024]{1,0:T(8,128)(2,1)} %param.16, s32[]{:T(128)S(6)} %select_n.107), kind=kOutput, calls=%fused_computation.138 | convolution fusion | flops 2684354560 | bytes 23330820 | tf_op jit(solution)/shard_map/dot_general | solution.py:84
  492.5 4.9 subtract_convert_fusion
  501.3 3.6 collective-permute-start.1
  505.8 2.8 fusion.5
  508.7 4.5 collective-permute-start.2
  514.0 2.9 fusion.6
  520.1 2.9 fusion.7
  523.0 2.6 fusion.48
  537.2 3.4 fusion.19
  549.5 16.6 %convolution_convert_fusion = bf16[2,4,256,5120]{3,2,1,0:T(8,128)(2,1)} fusion(bf16[512,5120]{1,0:T(8,128)(2,1)} %param.19, bf16[1,4,256,512]{3,2,1,0:T(8,128)(2,1)S(1)} %copy.97, bf16[1,4,256,512]{3,2,1,0:T(8,128)(2,1)S(1)} %copy.96), kind=kOutput, calls=%fused_computation.5 | convolution fusion | flops 10748952576 | bytes 28311552 | tf_op jit(solution)/shard_map/dot_general | solution.py:128
  566.1 34.6 %copy.148 = bf16[2,4,256,5120]{2,1,0,3:T(4,128)(2,1)} copy(bf16[2,4,256,5120]{3,2,1,0:T(8,128)(2,1)} %convolution_convert_fusion) | data formatting | bytes 41943040
  600.6 34.1 %reshape.656 = bf16[5120,2048]{1,0:T(8,128)(2,1)} reshape(bf16[5120,2,4,256]{3,2,1,0:T(4,128)(2,1)} %bitcast.462) | data formatting | bytes 41943040
  634.8 349.1 %reduce-scatter.4.cloned.1.call-done = bf16[640,2048]{1,0:T(8,128)(2,1)} async-done(((bf16[5120,2048]{1,0:T(8,128)(2,1)}), bf16[640,2048]{1,0:T(8,128)(2,1)}) %reduce-scatter.4.cloned.1.call-update) | async-done | bytes 2621456
  983.9 5.5 reshape.657
  989.4 5.6 copy.149
  995.0 2.4 add_convert_fusion
  (87 shorter events, 39.7 us)
Async XLA Ops:
  7.2 411.2 %all-gather.2.cloned.1.call-start = ((), (), s32[]{:S(2)}) async-start(), calls=%async_computation.1 | async-start | bytes 23592960 | tf_op jit(solution)/shard_map/all_gather | solution.py:78
  9.5 1.1 copy-start.5
  13.7 970.2 %reduce-scatter.4.cloned.1.call-start = ((), (), s32[]{:S(2)}) async-start(), calls=%async_computation.2 | async-start | bytes 23592960
  15.7 411.4 %copy-start.12 = (f32[5120]{0:T(1024)S(1)}, f32[5120]{0:T(1024)}, u32[]{:S(2)}) copy-start(f32[5120]{0:T(1024)} %param.13) | copy-start | bytes 61444
  439.2 8.9 copy-start
  439.2 8.9 copy-start.13
  490.4 10.9 %collective-permute-start = (bf16[2,4,256,128]{2,3,1,0:T(8,128)(2,1)S(1)}, bf16[2,4,256,128]{2,3,1,0:T(8,128)(2,1)S(1)}, u32[]{:S(2)}, u32[]{:S(2)}) collective-permute-start(bf16[2,4,256,128]{2,3,1,0:T(8,128)(2,1)S(1)} %pad_maximum_fusion.2), channel_id=1, source_target_pairs={{0,8},{8,16},{16,24},{1,9},{9,17},{17,25},{2,10},{10,18},{18,26},{... | collective-permute-start | bytes 1572872 | tf_op jit(solution)/shard_map/ppermute | solution.py:20
  501.3 32.2 %copy-start.7 = (bf16[2,4,256,128]{2,3,1,0:T(8,128)(2,1)}, bf16[2,4,256,128]{2,3,1,0:T(8,128)(2,1)S(1)}, u32[]{:S(2)}) copy-start(bf16[2,4,256,128]{2,3,1,0:T(8,128)(2,1)S(1)} %collective-permute-done) | copy-start | bytes 1572868
  501.3 7.4 collective-permute-start.1
  508.7 8.3 collective-permute-start.2
  516.9 17.8 %copy-start.9 = (bf16[2,4,256,128]{2,3,1,0:T(8,128)(2,1)}, bf16[2,4,256,128]{2,3,1,0:T(8,128)(2,1)S(1)}, u32[]{:S(2)}) copy-start(bf16[2,4,256,128]{2,3,1,0:T(8,128)(2,1)S(1)} %collective-permute-done.2) | copy-start | bytes 1572868
  525.5 2.1 copy-start.11
  537.2 3.5 copy-start.2
  537.2 4.7 copy-start.1
  543.0 1.3 copy-start.8
  544.3 2.2 copy-start.3
  544.3 2.3 copy-start.10
  544.3 3.0 copy-start.14
  634.8 360.2 %copy-start.4 = (bf16[4,256,640]{2,1,0:T(8,128)(2,1)S(1)}, bf16[4,256,640]{2,1,0:T(8,128)(2,1)}, u32[]{:S(2)}) copy-start(bf16[4,256,640]{2,1,0:T(8,128)(2,1)} %param.10) | copy-start | bytes 3932164
  634.8 360.2 %copy-start.6 = (bf16[1,4,256,640]{3,2,1,0:T(8,128)(2,1)S(1)}, bf16[1,4,256,640]{3,2,1,0:T(8,128)(2,1)}, u32[]{:S(2)}) copy-start(bf16[1,4,256,640]{3,2,1,0:T(8,128)(2,1)} %copy-done.5) | copy-start | bytes 3932164
Sparse Core Ops, SparseCore 0:
  13.8 404.4 all-gather.1
  634.9 348.9 reduce-scatter.3
where the time goes:
time: 1010 us
  waiting for transfers between devices  752 us (74%)
  local copies, waits for them, and re-layouts  102 us (10%)
  matrix products  79.6 us (8%)
  other arithmetic  47.9 us (5%)
  between operations  14.9 us (1%)
  starting transfers between devices  10.4 us (1%)
    all_gather x1, waiting for transfers between devices, per_device(): whole = lax.all_gather(streams, 'tp', axis=3, tiled=True)  403 us
    unnamed x3, waiting for transfers between devices  349 us
    unnamed x34, local copies, waits for them, and re-layouts  83 us
  transfers between devices with their start and end apart: 5, of which 2 were waited for; matrix products, arithmetic and copies ran while one was open for 2% of the time, Pallas kernels for 0%

commit v1 on v0

v1 whole, which is shorter than its diff:
```python
import functools
import math

import jax
import jax.numpy as jnp
from jax import lax
from jax.experimental import pallas as pl
from jax.experimental.pallas import tpu as pltpu
from jax.sharding import PartitionSpec as P

HD = 128
KVH = 8
BLOCK = 32
PAD = 16

eps = 1e-06
theta = 1000000.0
MESH = pl.DeviceIdType.MESH
VMEM_BYTES = 56 * 2**20


def tables(positions):
    half = HD // 2
    freqs = theta ** (-(jnp.arange(half).astype(jnp.float32) * 2.0) / HD)
    angles = positions[:, None] * freqs[None, :]
    cosine = jnp.cos(angles)
    sine = jnp.sin(angles)
    return jnp.concatenate([cosine, cosine], 1), jnp.concatenate([-sine, sine], 1)


def greet(groups):
    barrier = pltpu.get_barrier_semaphore()
    count = 0
    for axis, size in groups:
        me = lax.axis_index(axis)
        for step in range(1, size):
            pl.semaphore_signal(
                barrier, inc=1, device_id={axis: lax.rem(me + step, size)}, device_id_type=MESH
            )
        count += size - 1
    pl.semaphore_wait(barrier, count)


class Gather:
    def __init__(self, axis, lines, cross, own, out, send, recv, keep):
        self.axis, self.lines, self.cross = axis, lines, cross
        self.own, self.out, self.send, self.recv = own, out, send, recv
        me = lax.axis_index(axis)
        self.me, self.a, self.b = me, me // cross, lax.rem(me, cross)
        self.local = pltpu.make_async_copy(own, out.at[me], keep)
        self.started = []

    def copy(self, slot, way, device, src):
        return pltpu.make_async_remote_copy(
            src_ref=src,
            dst_ref=self.out.at[slot],
            send_sem=self.send.at[slot, way],
            recv_sem=self.recv.at[slot],
            device_id={self.axis: device},
            device_id_type=MESH,
        )

    def pass_on(self, slot, way, here, src=None):
        step = (self.cross, -self.cross, 1, -1)[way]
        inside = (
            self.a + 1 < self.lines, self.a > 0, self.b + 1 < self.cross, self.b > 0
        )[way]
        cond = inside if here is None else jnp.logical_and(here, inside)
        source = self.out.at[slot] if src is None else src

        @pl.when(cond)
        def _():
            self.copy(slot, way, self.me + step, source).start()

        self.started.append((slot, way, step, source, cond))

    def arrived(self, slot):
        self.copy(slot, 0, lax.rem(self.me + 1, self.lines * self.cross), self.out.at[slot]).wait_recv()

    def begin(self):
        for way in range(4):
            self.pass_on(self.me, way, None, self.own)
        self.local.start()

    def along(self, r):
        for sign in (-1, 1):
            src_a = self.a + sign * r
            here = src_a >= 0 if sign < 0 else src_a < self.lines
            slot = src_a * self.cross + self.b

            @pl.when(here)
            def _():
                self.arrived(slot)

            self.pass_on(slot, 0 if sign < 0 else 1, here)
            for way in (2, 3):
                self.pass_on(slot, way, here)

    def across(self):
        for r in range(1, self.cross):
            for sign in (-1, 1):
                src_b = self.b + sign * r
                here = src_b >= 0 if sign < 0 else src_b < self.cross
                for line in range(self.lines):
                    slot = line * self.cross + src_b

                    @pl.when(here)
                    def _():
                        self.arrived(slot)

                    if self.cross > 2:
                        self.pass_on(slot, 2 if sign < 0 else 3, here)

    def finish(self):
        for slot, way, step, source, cond in self.started:

            @pl.when(cond)
            def _():
                self.copy(slot, way, self.me + step, source).wait_send()

        self.local.wait()


def gather_kernel(axis, lines, cross, own, out, send, recv, keep):
    greet([(axis, lines * cross)])
    g = Gather(axis, lines, cross, own, out, send, recv, keep)
    g.begin()
    for r in range(1, lines):
        g.along(r)
    g.across()
    g.finish()


def gather(own, axis, lines, cross, collective_id):
    n = lines * cross
    return pl.pallas_call(
        functools.partial(gather_kernel, axis, lines, cross),
        out_shape=jax.ShapeDtypeStruct((n,) + own.shape, own.dtype),
        in_specs=[pl.BlockSpec(memory_space=pl.ANY)],
        out_specs=pl.BlockSpec(memory_space=pl.ANY),
        scratch_shapes=[
            pltpu.SemaphoreType.DMA((n, 4)),
            pltpu.SemaphoreType.DMA((n,)),
            pltpu.SemaphoreType.DMA,
        ],
        compiler_params=pltpu.CompilerParams(collective_id=collective_id, has_side_effects=True),
    )(own)


def first_kernel(
    tp, seq, lines, cross, own, weight, out, wout, send, recv, keep, wsend, wrecv, wkeep, xsend, xrecv
):
    greet([("tp", tp), ("seq", seq)])
    g = Gather("tp", lines, cross, own, out, send, recv, keep)
    g.begin()
    me = lax.axis_index("tp")
    s = lax.axis_index("seq")
    rows = weight.shape[1] // seq
    piece = pl.ds(pl.multiple_of(s * rows, rows), rows)

    def deal(d):
        to = lax.rem(me + d, tp)
        return pltpu.make_async_remote_copy(
            src_ref=weight.at[to, piece],
            dst_ref=wout.at[me, piece],
            send_sem=wsend.at[d],
            recv_sem=wrecv.at[d],
            device_id={"tp": to},
            device_id_type=MESH,
        )

    def share(d, e):
        source = lax.rem(me + tp - d, tp)
        return pltpu.make_async_remote_copy(
            src_ref=wout.at[source, piece],
            dst_ref=wout.at[source, piece],
            send_sem=xsend.at[d, e],
            recv_sem=xrecv.at[d, e],
            device_id={"seq": lax.rem(s + e, seq)},
            device_id_type=MESH,
        )

    own_weight = pltpu.make_async_copy(weight.at[me], wout.at[me], wkeep)
    own_weight.start()
    for d in range(1, tp):
        deal(d).start()
    g.along(1)
    for d in range(1, tp):
        deal(d).wait_recv()
        for e in range(1, seq):
            share(d, e).start()
    for r in range(2, lines):
        g.along(r)
    g.across()
    for d in range(1, tp):
        deal(d).wait_send()
        for e in range(1, seq):
            share(d, e).wait()
    own_weight.wait()
    g.finish()


def first_gather(own, weight, tp, seq, lines, cross):
    return pl.pallas_call(
        functools.partial(first_kernel, tp, seq, lines, cross),
        out_shape=(
            jax.ShapeDtypeStruct((tp,) + own.shape, own.dtype),
            jax.ShapeDtypeStruct(weight.shape, weight.dtype),
        ),
        in_specs=[pl.BlockSpec(memory_space=pl.ANY)] * 2,
        out_specs=(pl.BlockSpec(memory_space=pl.ANY),) * 2,
        scratch_shapes=[
            pltpu.SemaphoreType.DMA((tp, 4)),
            pltpu.SemaphoreType.DMA((tp,)),
            pltpu.SemaphoreType.DMA,
            pltpu.SemaphoreType.DMA((tp,)),
            pltpu.SemaphoreType.DMA((tp,)),
            pltpu.SemaphoreType.DMA,
            pltpu.SemaphoreType.DMA((tp, seq)),
            pltpu.SemaphoreType.DMA((tp, seq)),
        ],
        compiler_params=pltpu.CompilerParams(collective_id=0, has_side_effects=True),
    )(own, weight)


def spin(values, cosine, sine):
    parts = []
    for start in range(0, values.shape[1], HD):
        head = values[:, start : start + HD]
        parts.append(head * cosine + pltpu.roll(head, HD // 2, 1) * sine)
    return jnp.concatenate(parts, 1) if len(parts) > 1 else parts[0]


def project_kernel(
    tp, head_ref, x_ref, m_ref, mask_ref, gain_ref, qw, qb, kw, vw, vb, cos_ref, sin_ref,
    q_out, kvc_out, kvn_out, qm, km, vm,
):
    del head_ref
    width = x_ref.shape[2]
    q_cols = qw.shape[1]

    def project(ref):
        rows = ref.shape[1]
        total = jnp.zeros((rows, 1), jnp.float32)
        for t in range(tp):
            part = ref[t].astype(jnp.float32)
            total = total + jnp.sum(part * part, axis=1, keepdims=True)
        scale = lax.rsqrt(total / (tp * width) + eps)
        q = jnp.zeros((rows, q_cols), jnp.float32)
        k = jnp.zeros((rows, HD), jnp.float32)
        v = jnp.zeros((rows, HD), jnp.float32)
        for t in range(tp):
            here = pl.ds(t * width, width)
            normed = (ref[t].astype(jnp.float32) * scale * gain_ref[t]).astype(jnp.bfloat16)
            q = q + jnp.dot(normed, qw[here, :], preferred_element_type=jnp.float32)
            k = k + jnp.dot(normed, kw[here, :], preferred_element_type=jnp.float32)
            v = v + jnp.dot(normed, vw[here, :], preferred_element_type=jnp.float32)
        return q + qb[...], k, v + vb[0]

    @pl.when(pl.program_id(0) == 0)
    def _():
        qm[...], km[...], vm[...] = project(m_ref)

    cosine, sine = cos_ref[...], sin_ref[...]
    rows = x_ref.shape[1]
    q, k, v = project(x_ref)
    q = spin(q, cosine, sine)
    k = spin(k, cosine, sine)
    masked = mask_ref[...] == 1
    q_mask = spin(jnp.broadcast_to(qm[0:1, :], (rows, q_cols)), cosine, sine)
    k_mask = spin(jnp.broadcast_to(km[0:1, :], (rows, HD)), cosine, sine)
    v_mask = jnp.broadcast_to(vm[0:1, :], (rows, HD))
    q_out[0] = q.astype(jnp.bfloat16)
    q_out[1] = jnp.where(masked, q_mask, q).astype(jnp.bfloat16)
    kvc_out[0] = k.astype(jnp.bfloat16)
    kvc_out[1] = v.astype(jnp.bfloat16)
    kvn_out[0] = jnp.where(masked, k_mask, k).astype(jnp.bfloat16)
    kvn_out[1] = jnp.where(masked, v_mask, v).astype(jnp.bfloat16)


def project(head, whole, mask_col, gain, q_weight, q_bias, k_weight, v_weight, v_bias, cosine, sine):
    tp, padded, width = whole.shape
    tokens = cosine.shape[0]
    rows = padded - PAD
    d_model, q_cols = q_weight.shape
    fixed = lambda *shape: pl.BlockSpec(shape, lambda i, h: (0,) * len(shape))
    return pl.pallas_call(
        functools.partial(project_kernel, tp),
        out_shape=(
            jax.ShapeDtypeStruct((2, rows, q_cols), jnp.bfloat16),
            jax.ShapeDtypeStruct((2, rows, HD), jnp.bfloat16),
            jax.ShapeDtypeStruct((2, rows, HD), jnp.bfloat16),
        ),
        grid_spec=pltpu.PrefetchScalarGridSpec(
            num_scalar_prefetch=1,
            grid=(rows // tokens,),
            in_specs=[
                pl.BlockSpec((tp, tokens, width), lambda i, h: (0, i, 0)),
                pl.BlockSpec((tp, PAD, width), lambda i, h: (0, rows // PAD, 0)),
                pl.BlockSpec((tokens, 1), lambda i, h: (i, 0)),
                fixed(tp, 1, width),
                fixed(d_model, q_cols),
                fixed(1, q_cols),
                pl.BlockSpec((d_model, HD), lambda i, h: (0, h[0])),
                pl.BlockSpec((d_model, HD), lambda i, h: (0, h[0])),
                pl.BlockSpec((1, 1, HD), lambda i, h: (h[0], 0, 0)),
                fixed(tokens, HD),
                fixed(tokens, HD),
            ],
            out_specs=(
                pl.BlockSpec((2, tokens, q_cols), lambda i, h: (0, i, 0)),
                pl.BlockSpec((2, tokens, HD), lambda i, h: (0, i, 0)),
                pl.BlockSpec((2, tokens, HD), lambda i, h: (0, i, 0)),
            ),
            scratch_shapes=[
                pltpu.VMEM((PAD, q_cols), jnp.float32),
                pltpu.VMEM((PAD, HD), jnp.float32),
                pltpu.VMEM((PAD, HD), jnp.float32),
            ],
        ),
        compiler_params=pltpu.CompilerParams(vmem_limit_bytes=VMEM_BYTES),
    )(
        head, whole, whole, mask_col, gain.reshape(tp, 1, width), q_weight, q_bias.reshape(1, -1),
        k_weight, v_weight, v_bias.reshape(-1, 1, HD), cosine, sine,
    )


def attend_kernel(seq_ref, q_ref, kv_ref, kvn_ref, out_ref):
    seq, _, tokens, _ = kv_ref.shape
    heads = q_ref.shape[2] // HD
    keys = seq * tokens
    k_all = kv_ref[:, 0].reshape(keys, HD)
    v_all = kv_ref[:, 1].reshape(keys, HD)
    k_own, v_own = kvn_ref[0], kvn_ref[1]
    scale = 1.0 / math.sqrt(HD)

    def blocks(count, axis, start):
        return (start + lax.broadcasted_iota(jnp.int32, (tokens, count), axis)) // BLOCK

    q_block = blocks(keys, 0, seq_ref[0] * tokens)
    k_block = blocks(keys, 1, 0)
    clean_bias = jnp.where(k_block <= q_block, 0.0, -1e30)
    noisy_bias = jnp.where(k_block < q_block, 0.0, -1e30)
    own_bias = jnp.where(blocks(tokens, 1, 0) == blocks(tokens, 0, 0), 0.0, -1e30)

    def scores(q, k, bias):
        dims = (((1,), (1,)), ((), ()))
        return lax.dot_general(q, k, dims, preferred_element_type=jnp.float32) * scale + bias

    def weigh(expo, v):
        return jnp.dot(expo.astype(jnp.bfloat16), v, preferred_element_type=jnp.float32)

    for h in range(heads):
        cols = pl.ds(h * HD, HD)
        s = scores(q_ref[0, :, cols], k_all, clean_bias)
        expo = jnp.exp(s - jnp.max(s, axis=1, keepdims=True))
        denom = jnp.sum(expo, axis=1, keepdims=True)
        out_ref[0, :, cols] = (weigh(expo, v_all) / denom).astype(jnp.bfloat16)
        q = q_ref[1, :, cols]
        s = scores(q, k_all, noisy_bias)
        t = scores(q, k_own, own_bias)
        best = jnp.maximum(jnp.max(s, axis=1, keepdims=True), jnp.max(t, axis=1, keepdims=True))
        expo_s, expo_t = jnp.exp(s - best), jnp.exp(t - best)
        denom = jnp.sum(expo_s, axis=1, keepdims=True) + jnp.sum(expo_t, axis=1, keepdims=True)
        total = weigh(expo_s, v_all) + weigh(expo_t, v_own)
        out_ref[1, :, cols] = (total / denom).astype(jnp.bfloat16)


def attend(my_seq, queries, kv_clean, kv_noisy, tokens):
    seq = kv_clean.shape[0]
    _, rows, q_cols = queries.shape
    return pl.pallas_call(
        attend_kernel,
        out_shape=jax.ShapeDtypeStruct((2, rows, q_cols), jnp.bfloat16),
        grid_spec=pltpu.PrefetchScalarGridSpec(
            num_scalar_prefetch=1,
            grid=(rows // tokens,),
            in_specs=[
                pl.BlockSpec((2, tokens, q_cols), lambda i, s: (0, i, 0)),
                pl.BlockSpec((seq, 2, tokens, HD), lambda i, s: (0, 0, i, 0)),
                pl.BlockSpec((2, tokens, HD), lambda i, s: (0, i, 0)),
            ],
            out_specs=pl.BlockSpec((2, tokens, q_cols), lambda i, s: (0, i, 0)),
        ),
        compiler_params=pltpu.CompilerParams(vmem_limit_bytes=VMEM_BYTES),
    )(my_seq, queries, kv_clean, kv_noisy)


def combine_kernel(a_ref, w_ref, x_ref, mask_ref, embed_ref, clean_ref, noisy_ref):
    tp = a_ref.shape[0]
    clean = x_ref[0].astype(jnp.float32)
    noisy = jnp.where(mask_ref[...] == 1, embed_ref[...].astype(jnp.float32), clean)
    for stream, base, out in ((0, clean, clean_ref), (1, noisy, noisy_ref)):
        total = jnp.zeros(base.shape, jnp.float32)
        for t in range(tp):
            total = total + jnp.dot(a_ref[t, stream], w_ref[t], preferred_element_type=jnp.float32)
        out[0] = (base + total).astype(jnp.bfloat16)


def combine(attended, weight, clean_in, mask_col, mask_embed):
    tp, _, rows, q_cols = attended.shape
    docs, tokens, width = clean_in.shape
    block = pl.BlockSpec((1, tokens, width), lambda i: (i, 0, 0))
    out = jax.ShapeDtypeStruct(clean_in.shape, jnp.bfloat16)
    return pl.pallas_call(
        combine_kernel,
        out_shape=(out, out),
        grid=(docs,),
        in_specs=[
            pl.BlockSpec((tp, 2, tokens, q_cols), lambda i: (0, 0, i, 0)),
            pl.BlockSpec((tp, q_cols, width), lambda i: (0, 0, 0)),
            block,
            pl.BlockSpec((tokens, 1), lambda i: (i, 0)),
            pl.BlockSpec((1, width), lambda i: (0, 0)),
        ],
        out_specs=(block, block),
        compiler_params=pltpu.CompilerParams(vmem_limit_bytes=VMEM_BYTES),
    )(attended, weight, clean_in, mask_col, mask_embed.reshape(1, width))


def per_device(
    tp,
    seq,
    clean_in,
    noise_mask,
    mask_embed,
    norm_gain,
    q_weight,
    q_bias,
    k_weight,
    v_weight,
    v_bias,
    o_weight,
):
    docs, tokens, width = clean_in.shape
    q_cols = q_weight.shape[1]
    rows = docs * tokens
    lines = 4 if tp % 4 == 0 else 1
    cross = tp // lines
    seq_cross = 2 if seq % 2 == 0 else 1
    my_seq = lax.axis_index("seq")
    head = lax.axis_index("tp") * KVH // tp
    mask_col = noise_mask.reshape(rows, 1)
    own = jnp.concatenate(
        [clean_in.reshape(rows, width), jnp.broadcast_to(mask_embed[None, :], (PAD, width))], 0
    )
    dealt = jnp.transpose(o_weight.reshape(q_cols, tp, width), (1, 0, 2))
    whole, out_weight = first_gather(own, dealt, tp, seq, lines, cross)
    positions = (my_seq * tokens + jnp.arange(tokens)).astype(jnp.float32)
    cosine, sine = tables(positions)
    queries, kv_clean, kv_noisy = project(
        head.reshape(1), whole, mask_col, norm_gain, q_weight, q_bias, k_weight, v_weight, v_bias,
        cosine, sine,
    )
    kv_all = gather(kv_clean, "seq", seq // seq_cross, seq_cross, 1)
    attended = attend(my_seq.reshape(1), queries, kv_all, kv_noisy, tokens)
    spread = gather(attended, "tp", lines, cross, 2)
    return combine(spread, out_weight, clean_in, mask_col, mask_embed)


def solution(mesh):
    return jax.shard_map(
        functools.partial(per_device, mesh.shape["tp"], mesh.shape["seq"]),
        mesh=mesh,
        in_specs=(
            P(None, "seq", "tp"),
            P(None, "seq"),
            P("tp"),
            P(),
            P(None, "tp"),
            P("tp"),
            P(),
            P(),
            P(),
            P("tp", None),
        ),
        out_specs=(P(None, "seq", "tp"), P(None, "seq", "tp")),
        check_vma=False,
    )
```

time: 1010 us -> 446 us (0.44)
  waiting for transfers between devices: 752 us -> 0 us
  Pallas kernels: 0 us -> 421 us
  local copies, waits for them, and re-layouts: 102 us -> 19.5 us
  matrix products: 79.6 us -> 0 us
  other arithmetic: 47.9 us -> 3.93 us
  between operations: 14.9 us -> 0.69 us
  starting transfers between devices: 10.4 us -> 0 us
    pallas_call x0 -> x6, Pallas kernels: none -> 421 us  [the longest x2 206 us: gather(): pl.pallas_call(functools.partial(gather_kernel, axis, lines, cross), out_...]
    all_gather x1 -> x0, waiting for transfers between devices: 403 us -> none  [per_device(): whole = lax.all_gather(streams, 'tp', axis=3, tiled=True)]
    unnamed x3 -> x0, waiting for transfers between devices: 349 us -> none
    dot_general x22 -> x0, matrix products: 79.6 us -> none  [the longest x1 16.6 us: per_device(): jnp.dot(attended.reshape(-1, q_cols), o_weight, preferred_element_type=jn...]
    unnamed x34 -> x3, local copies, waits for them, and re-layouts: 83 us -> 9.66 us
    reduce_sum x10 -> x0, other arithmetic: 20.8 us -> none  [the longest x9 12 us: update(): denom = denom * factor + jnp.sum(expo, axis=-1)]
    convert_element_type x2 -> x1, other arithmetic: 14.4 us -> 0.01 us  [per_device(): positions = (my_seq * tokens + jnp.arange(tokens)).astype(jnp.float32)]
    ppermute x3 -> x0, starting transfers between devices: 10.3 us -> none  [from_behind(): return lax.ppermute(block, axis, route)]
  transfers between devices with their start and end apart: 5 -> 0, of which waited for: 2 -> 0; matrix products, arithmetic and copies ran while one was open for 2% -> 0% of each run, Pallas kernels for 0% -> 0%
where the time goes in v1:
time: 446 us; the launch traced here: 445 us
  Pallas kernels  421 us (94%)
  local copies, waits for them, and re-layouts  19.5 us (4%)
    pallas_call x2, Pallas kernels, gather(): pl.pallas_call(functools.partial(gather_kernel, axis, lines, cross), out_...  206 us
    pallas_call x1, Pallas kernels, first_gather(): pl.pallas_call(functools.partial(first_kernel, tp, seq, lines, cross), ou...  153 us
    pallas_call x1, Pallas kernels, project(): pl.pallas_call(functools.partial(project_kernel, tp), out_shape=(jax.Shap...  21.7 us
    pallas_call x1, Pallas kernels, attend(): pl.pallas_call(attend_kernel, out_shape=jax.ShapeDtypeStruct((2, rows, q_...  21.4 us
    pallas_call x1, Pallas kernels, combine(): pl.pallas_call(combine_kernel, out_shape=(out, out), grid=(docs,), in_spe...  18.7 us
    unnamed x3, local copies, waits for them, and re-layouts  9.66 us

profile of v1, /device:TPU:0, one launch (start us, length us, event | category | flops | bytes accessed | tf_op | source)
XLA Modules:
  0.0 444.9 jit_solution(7082340260281877435)
XLA Ops:
  0.7 1.3 broadcast_in_dim.5.embed_ref
  1.9 0.7 copy.16
  2.6 0.7 broadcast_in_dim.4
  3.3 0.5 fusion
  3.9 0.8 pad_maximum_fusion.1
  4.7 1.0 copy.17
  5.7 2.5 pad_maximum_fusion.own
  8.2 8.0 %copy.12 = bf16[512,5120]{0,1:T(8,128)(2,1)} copy(bf16[512,5120]{1,0:T(8,128)(2,1)} %param.19) | data formatting | bytes 10485760 | tf_op args[9]
  16.2 7.9 %copy.13 = bf16[512,8,640]{2,0,1:T(8,128)(2,1)} copy(bf16[512,8,640]{0,2,1:T(8,128)(2,1)} %bitcast.13) | data formatting | bytes 10485760 | tf_op jit(solution)/shard_map/reshape | solution.py:447
  24.1 153.3 %shard_map.113 = (bf16[8,1040,640]{2,1,0:T(8,128)(2,1)}, bf16[8,512,640]{2,1,0:T(8,128)(2,1)}) custom-call(bf16[1040,640]{1,0:T(8,128)(2,1)} %pad_maximum_fusion.own, bf16[8,512,640]{2,1,0:T(8,128)(2,1)} %bitcast.12), custom_call_target="tpu_custom_call" | custom-call | tf_op jit(solution)/shard_map/pallas_call | solution.py:204
  177.4 21.7 %shard_map.114 = (bf16[2,1024,512]{2,1,0:T(8,128)(2,1)}, bf16[2,1024,128]{2,1,0:T(8,128)(2,1)}, bf16[2,1024,128]{2,1,0:T(8,128)(2,1)}) custom-call(s32[1]{0:T(128)} %bitcast.1.head_ref, bf16[8,1040,640]{2,1,0:T(8,128)(2,1)} %get-tuple-element.7.x_ref.m_ref, bf16[8,1040,640]{2,1,0:T(8,128)(2,1)} %get-tuple-element.7.x_ref.m_ref, s32[1024,1]{1,0:T(8,128)} %bitcast.15, ...), custom_call_target="tpu_custom_call" | custom-call | tf_op jit(solution)/shard_map/pallas_call | solution.py:287
  199.1 17.2 %shard_map.115.kv_ref = bf16[4,2,1024,128]{3,2,1,0:T(8,128)(2,1)} custom-call(bf16[2,1024,128]{2,1,0:T(8,128)(2,1)} %get-tuple-element.9.own), custom_call_target="tpu_custom_call" | custom-call | tf_op jit(solution)/shard_map/pallas_call | solution.py:136
  216.3 21.4 %shard_map.116.own = bf16[2,1024,512]{2,1,0:T(8,128)(2,1)} custom-call(s32[1]{0:T(128)} %bitcast.seq_ref, bf16[2,1024,512]{2,1,0:T(8,128)(2,1)} %get-tuple-element.8.q_ref, bf16[4,2,1024,128]{3,2,1,0:T(8,128)(2,1)} %shard_map.115.kv_ref, bf16[2,1024,128]{2,1,0:T(8,128)(2,1)} %get-tuple-element.10.kvn_ref), custom_call_target="tpu_custom_call" | custom-call | tf_op jit(solution)/shard_map/pallas_call | solution.py:372
  237.7 188.5 %shard_map.117.a_ref = bf16[8,2,1024,512]{3,2,1,0:T(8,128)(2,1)} custom-call(bf16[2,1024,512]{2,1,0:T(8,128)(2,1)} %shard_map.116.own), custom_call_target="tpu_custom_call" | custom-call | tf_op jit(solution)/shard_map/pallas_call | solution.py:136
  426.2 18.7 %shard_map.118 = (bf16[4,256,640]{2,1,0:T(8,128)(2,1)}, bf16[4,256,640]{2,1,0:T(8,128)(2,1)}) custom-call(bf16[8,2,1024,512]{3,2,1,0:T(8,128)(2,1)} %shard_map.117.a_ref, bf16[8,512,640]{2,1,0:T(8,128)(2,1)} %get-tuple-element.11.w_ref, bf16[4,256,640]{2,1,0:T(8,128)(2,1)} %x_ref.1, s32[1024,1]{1,0:T(8,128)} %bitcast.16, ...), custom_call_target="tpu_custom_call" | custom-call | tf_op jit(solution)/shard_map/pallas_call | solution.py:405
  (2 shorter events, 0.0 us)

commit v2 on v1

--- a/solution.py
+++ b/solution.py
@@ -16,7 +16,7 @@
 eps = 1e-06
 theta = 1000000.0
 MESH = pl.DeviceIdType.MESH
-VMEM_BYTES = 56 * 2**20
+VMEM_BYTES = 60 * 2**20
 
 
 def tables(positions):
@@ -153,24 +153,24 @@
     greet([("tp", tp), ("seq", seq)])
     g = Gather("tp", lines, cross, own, out, send, recv, keep)
     g.begin()
-    me = lax.axis_index("tp")
     s = lax.axis_index("seq")
-    rows = weight.shape[1] // seq
+    rows = weight.shape[0] // seq
+    cols = weight.shape[1] // lines
     piece = pl.ds(pl.multiple_of(s * rows, rows), rows)
 
     def deal(d):
-        to = lax.rem(me + d, tp)
+        to = lax.rem(g.a + d, lines)
         return pltpu.make_async_remote_copy(
-            src_ref=weight.at[to, piece],
-            dst_ref=wout.at[me, piece],
+            src_ref=weight.at[piece, pl.ds(pl.multiple_of(to * cols, 128), cols)],
+            dst_ref=wout.at[g.a, piece],
             send_sem=wsend.at[d],
             recv_sem=wrecv.at[d],
-            device_id={"tp": to},
+            device_id={"tp": to * cross + g.b},
             device_id_type=MESH,
         )
 
     def share(d, e):
-        source = lax.rem(me + tp - d, tp)
+        source = lax.rem(g.a + lines - d, lines)
         return pltpu.make_async_remote_copy(
             src_ref=wout.at[source, piece],
             dst_ref=wout.at[source, piece],
@@ -180,19 +180,21 @@
             device_id_type=MESH,
         )
 
-    own_weight = pltpu.make_async_copy(weight.at[me], wout.at[me], wkeep)
+    own_weight = pltpu.make_async_copy(
+        weight.at[:, pl.ds(pl.multiple_of(g.a * cols, 128), cols)], wout.at[g.a], wkeep
+    )
     own_weight.start()
-    for d in range(1, tp):
+    for d in range(1, lines):
         deal(d).start()
     g.along(1)
-    for d in range(1, tp):
+    for d in range(1, lines):
         deal(d).wait_recv()
         for e in range(1, seq):
             share(d, e).start()
     for r in range(2, lines):
         g.along(r)
     g.across()
-    for d in range(1, tp):
+    for d in range(1, lines):
         deal(d).wait_send()
         for e in range(1, seq):
             share(d, e).wait()
@@ -201,11 +203,12 @@
 
 
 def first_gather(own, weight, tp, seq, lines, cross):
+    q_cols, d_model = weight.shape
     return pl.pallas_call(
         functools.partial(first_kernel, tp, seq, lines, cross),
         out_shape=(
             jax.ShapeDtypeStruct((tp,) + own.shape, own.dtype),
-            jax.ShapeDtypeStruct(weight.shape, weight.dtype),
+            jax.ShapeDtypeStruct((lines, q_cols, d_model // lines), weight.dtype),
         ),
         in_specs=[pl.BlockSpec(memory_space=pl.ANY)] * 2,
         out_specs=(pl.BlockSpec(memory_space=pl.ANY),) * 2,
@@ -213,11 +216,11 @@
             pltpu.SemaphoreType.DMA((tp, 4)),
             pltpu.SemaphoreType.DMA((tp,)),
             pltpu.SemaphoreType.DMA,
-            pltpu.SemaphoreType.DMA((tp,)),
-            pltpu.SemaphoreType.DMA((tp,)),
+            pltpu.SemaphoreType.DMA((lines,)),
+            pltpu.SemaphoreType.DMA((lines,)),
             pltpu.SemaphoreType.DMA,
-            pltpu.SemaphoreType.DMA((tp, seq)),
-            pltpu.SemaphoreType.DMA((tp, seq)),
+            pltpu.SemaphoreType.DMA((lines, seq)),
+            pltpu.SemaphoreType.DMA((lines, seq)),
         ],
         compiler_params=pltpu.CompilerParams(collective_id=0, has_side_effects=True),
     )(own, weight)
@@ -325,19 +328,23 @@
     )
 
 
-def attend_kernel(seq_ref, q_ref, kv_ref, kvn_ref, out_ref):
-    seq, _, tokens, _ = kv_ref.shape
-    heads = q_ref.shape[2] // HD
+def finish_kernel(
+    tp, lines, cross, q_ref, kv_ref, kvn_ref, w_ref, x_ref, mask_ref, embed_ref, clean_ref, noisy_ref,
+    heads_ref, total_ref, leave_ref, come_ref, send, recv, psend, precv,
+):
+    greet([("tp", tp)])
+    me = lax.axis_index("tp")
+    a, b = me // cross, lax.rem(me, cross)
+    seq, _, docs, tokens, _ = kv_ref.shape
+    q_cols = q_ref.shape[3]
+    width = x_ref.shape[2]
     keys = seq * tokens
-    k_all = kv_ref[:, 0].reshape(keys, HD)
-    v_all = kv_ref[:, 1].reshape(keys, HD)
-    k_own, v_own = kvn_ref[0], kvn_ref[1]
     scale = 1.0 / math.sqrt(HD)
 
     def blocks(count, axis, start):
         return (start + lax.broadcasted_iota(jnp.int32, (tokens, count), axis)) // BLOCK
 
-    q_block = blocks(keys, 0, seq_ref[0] * tokens)
+    q_block = blocks(keys, 0, lax.axis_index("seq") * tokens)
     k_block = blocks(keys, 1, 0)
     clean_bias = jnp.where(k_block <= q_block, 0.0, -1e30)
     noisy_bias = jnp.where(k_block < q_block, 0.0, -1e30)
@@ -350,72 +357,155 @@
     def weigh(expo, v):
         return jnp.dot(expo.astype(jnp.bfloat16), v, preferred_element_type=jnp.float32)
 
-    for h in range(heads):
-        cols = pl.ds(h * HD, HD)
-        s = scores(q_ref[0, :, cols], k_all, clean_bias)
-        expo = jnp.exp(s - jnp.max(s, axis=1, keepdims=True))
-        denom = jnp.sum(expo, axis=1, keepdims=True)
-        out_ref[0, :, cols] = (weigh(expo, v_all) / denom).astype(jnp.bfloat16)
-        q = q_ref[1, :, cols]
-        s = scores(q, k_all, noisy_bias)
-        t = scores(q, k_own, own_bias)
-        best = jnp.maximum(jnp.max(s, axis=1, keepdims=True), jnp.max(t, axis=1, keepdims=True))
-        expo_s, expo_t = jnp.exp(s - best), jnp.exp(t - best)
-        denom = jnp.sum(expo_s, axis=1, keepdims=True) + jnp.sum(expo_t, axis=1, keepdims=True)
-        total = weigh(expo_s, v_all) + weigh(expo_t, v_own)
-        out_ref[1, :, cols] = (total / denom).astype(jnp.bfloat16)
-
-
-def attend(my_seq, queries, kv_clean, kv_noisy, tokens):
-    seq = kv_clean.shape[0]
-    _, rows, q_cols = queries.shape
+    def pass_on(d, slot, way):
+        return pltpu.make_async_remote_copy(
+            src_ref=heads_ref.at[d, slot],
+            dst_ref=heads_ref.at[d, slot],
+            send_sem=send.at[d, slot, way],
+            recv_sem=recv.at[d, slot],
+            device_id={"tp": lax.rem(me + (cross, tp - cross)[way], tp)},
+            device_id_type=MESH,
+        )
+
+    more = (a + 1 < lines, a > 0)
+
+    def attend(d, carry):
+        k_all = kv_ref[:, 0, d].reshape(keys, HD)
+        v_all = kv_ref[:, 1, d].reshape(keys, HD)
+        k_own, v_own = kvn_ref[0, d], kvn_ref[1, d]
+        for h in range(q_cols // HD):
+            cols = pl.ds(h * HD, HD)
+            s = scores(q_ref[0, d, :, cols], k_all, clean_bias)
+            expo = jnp.exp(s - jnp.max(s, axis=1, keepdims=True))
+            denom = jnp.sum(expo, axis=1, keepdims=True)
+            heads_ref[d, a, 0, :, cols] = (weigh(expo, v_all) / denom).astype(jnp.bfloat16)
+            q = q_ref[1, d, :, cols]
+            s = scores(q, k_all, noisy_bias)
+            t = scores(q, k_own, own_bias)
+            best = jnp.maximum(jnp.max(s, axis=1, keepdims=True), jnp.max(t, axis=1, keepdims=True))
+            expo_s, expo_t = jnp.exp(s - best), jnp.exp(t - best)
+            denom = jnp.sum(expo_s, axis=1, keepdims=True) + jnp.sum(expo_t, axis=1, keepdims=True)
+            total = weigh(expo_s, v_all) + weigh(expo_t, v_own)
+            heads_ref[d, a, 1, :, cols] = (total / denom).astype(jnp.bfloat16)
+        for way in range(2):
+
+            @pl.when(more[way])
+            def _():
+                pass_on(d, a, way).start()
+
+        return carry
+
+    lax.fori_loop(0, docs, attend, 0)
+
+    def along(r, d):
+        for way, here, slot in ((0, a - r >= 0, a - r), (1, a + r < lines, a + r)):
+
+            @pl.when(here)
+            def _():
+                pass_on(d, slot, way).wait_recv()
+
+            @pl.when(jnp.logical_and(here, more[way]))
+            def _():
+                pass_on(d, slot, way).start()
+
+    for r in range(1, lines - 1):
+        lax.fori_loop(0, docs, lambda d, carry: (along(r, d), carry)[1], 0)
+
+    def partial(d, e):
+        return pltpu.make_async_remote_copy(
+            src_ref=leave_ref.at[d, e],
+            dst_ref=come_ref.at[d, e],
+            send_sem=psend.at[d, e],
+            recv_sem=precv.at[d, e],
+            device_id={"tp": a * cross + lax.rem(b + e, cross)},
+            device_id_type=MESH,
+        )
+
+    def multiply(d, carry):
+        along(lines - 1, d)
+        for stream in range(2):
+            total = jnp.zeros((tokens, cross * width), jnp.float32)
+            for line in range(lines):
+                total = total + jnp.dot(
+                    heads_ref[d, line, stream], w_ref[line], preferred_element_type=jnp.float32
+                )
+            for target in range(cross):
+                part = total[:, target * width : (target + 1) * width]
+
+                @pl.when(b == target)
+                def _():
+                    total_ref[d, stream] = part
+
+                @pl.when(b != target)
+                def _():
+                    leave_ref[d, lax.rem(target - b + cross, cross), stream] = part.astype(
+                        jnp.bfloat16
+                    )
+
+        for e in range(1, cross):
+            partial(d, e).start()
+        return carry
+
+    lax.fori_loop(0, docs, multiply, 0)
+
+    def close(d, carry):
+        clean = x_ref[d].astype(jnp.float32)
+        noisy = jnp.where(mask_ref[d] == 1, embed_ref[...].astype(jnp.float32), clean)
+        for e in range(1, cross):
+            partial(d, e).wait_recv()
+        for stream, base, out in ((0, clean, clean_ref), (1, noisy, noisy_ref)):
+            total = total_ref[d, stream]
+            for e in range(1, cross):
+                total = total + come_ref[d, e, stream].astype(jnp.float32)
+            out[d] = (base + total).astype(jnp.bfloat16)
+        for e in range(1, cross):
+            partial(d, e).wait_send()
+        for r in range(lines):
+            for way, here, slot in ((0, a - r >= 0, a - r), (1, a + r < lines, a + r)):
+
+                @pl.when(jnp.logical_and(here, more[way]))
+                def _():
+                    pass_on(d, slot, way).wait_send()
+
+        return carry
+
+    lax.fori_loop(0, docs, close, 0)
+
+
+def finish(queries, kv_all, kv_noisy, weight, clean_in, mask_col, mask_embed, tp, lines, cross):
+    docs, tokens, width = clean_in.shape
+    q_cols = queries.shape[2]
+    seq = kv_all.shape[0]
+    out = jax.ShapeDtypeStruct(clean_in.shape, jnp.bfloat16)
+    vmem = pl.BlockSpec(memory_space=pltpu.VMEM)
+    dma = pltpu.SemaphoreType.DMA
     return pl.pallas_call(
-        attend_kernel,
-        out_shape=jax.ShapeDtypeStruct((2, rows, q_cols), jnp.bfloat16),
-        grid_spec=pltpu.PrefetchScalarGridSpec(
-            num_scalar_prefetch=1,
-            grid=(rows // tokens,),
-            in_specs=[
-                pl.BlockSpec((2, tokens, q_cols), lambda i, s: (0, i, 0)),
-                pl.BlockSpec((seq, 2, tokens, HD), lambda i, s: (0, 0, i, 0)),
-                pl.BlockSpec((2, tokens, HD), lambda i, s: (0, i, 0)),
-            ],
-            out_specs=pl.BlockSpec((2, tokens, q_cols), lambda i, s: (0, i, 0)),
+        functools.partial(finish_kernel, tp, lines, cross),
+        out_shape=(out, out),
+        in_specs=[vmem] * 7,
+        out_specs=(vmem, vmem),
+        scratch_shapes=[
+            pltpu.VMEM((docs, lines, 2, tokens, q_cols), jnp.bfloat16),
+            pltpu.VMEM((docs, 2, tokens, width), jnp.float32),
+            pltpu.VMEM((docs, cross, 2, tokens, width), jnp.bfloat16),
+            pltpu.VMEM((docs, cross, 2, tokens, width), jnp.bfloat16),
+            dma((docs, lines, 2)),
+            dma((docs, lines)),
+            dma((docs, cross)),
+            dma((docs, cross)),
+        ],
+        compiler_params=pltpu.CompilerParams(
+            collective_id=2, has_side_effects=True, vmem_limit_bytes=VMEM_BYTES
         ),
-        compiler_params=pltpu.CompilerParams(vmem_limit_bytes=VMEM_BYTES),
-    )(my_seq, queries, kv_clean, kv_noisy)
-
-
-def combine_kernel(a_ref, w_ref, x_ref, mask_ref, embed_ref, clean_ref, noisy_ref):
-    tp = a_ref.shape[0]
-    clean = x_ref[0].astype(jnp.float32)
-    noisy = jnp.where(mask_ref[...] == 1, embed_ref[...].astype(jnp.float32), clean)
-    for stream, base, out in ((0, clean, clean_ref), (1, noisy, noisy_ref)):
-        total = jnp.zeros(base.shape, jnp.float32)
-        for t in range(tp):
-            total = total + jnp.dot(a_ref[t, stream], w_ref[t], preferred_element_type=jnp.float32)
-        out[0] = (base + total).astype(jnp.bfloat16)
-
-
-def combine(attended, weight, clean_in, mask_col, mask_embed):
-    tp, _, rows, q_cols = attended.shape
-    docs, tokens, width = clean_in.shape
-    block = pl.BlockSpec((1, tokens, width), lambda i: (i, 0, 0))
-    out = jax.ShapeDtypeStruct(clean_in.shape, jnp.bfloat16)
-    return pl.pallas_call(
-        combine_kernel,
-        out_shape=(out, out),
-        grid=(docs,),
-        in_specs=[
-            pl.BlockSpec((tp, 2, tokens, q_cols), lambda i: (0, 0, i, 0)),
-            pl.BlockSpec((tp, q_cols, width), lambda i: (0, 0, 0)),
-            block,
-            pl.BlockSpec((tokens, 1), lambda i: (i, 0)),
-            pl.BlockSpec((1, width), lambda i: (0, 0)),
-        ],
-        out_specs=(block, block),
-        compiler_params=pltpu.CompilerParams(vmem_limit_bytes=VMEM_BYTES),
-    )(attended, weight, clean_in, mask_col, mask_embed.reshape(1, width))
+    )(
+        queries.reshape(2, docs, tokens, q_cols),
+        kv_all.reshape(seq, 2, docs, tokens, HD),
+        kv_noisy.reshape(2, docs, tokens, HD),
+        weight,
+        clean_in,
+        mask_col.reshape(docs, tokens, 1),
+        mask_embed.reshape(1, width),
+    )
 
 
 def per_device(
@@ -433,7 +523,6 @@
     o_weight,
 ):
     docs, tokens, width = clean_in.shape
-    q_cols = q_weight.shape[1]
     rows = docs * tokens
     lines = 4 if tp % 4 == 0 else 1
     cross = tp // lines
@@ -444,8 +533,7 @@
     own = jnp.concatenate(
         [clean_in.reshape(rows, width), jnp.broadcast_to(mask_embed[None, :], (PAD, width))], 0
     )
-    dealt = jnp.transpose(o_weight.reshape(q_cols, tp, width), (1, 0, 2))
-    whole, out_weight = first_gather(own, dealt, tp, seq, lines, cross)
+    whole, out_weight = first_gather(own, o_weight, tp, seq, lines, cross)
     positions = (my_seq * tokens + jnp.arange(tokens)).astype(jnp.float32)
     cosine, sine = tables(positions)
     queries, kv_clean, kv_noisy = project(
@@ -453,9 +541,9 @@
         cosine, sine,
     )
     kv_all = gather(kv_clean, "seq", seq // seq_cross, seq_cross, 1)
-    attended = attend(my_seq.reshape(1), queries, kv_all, kv_noisy, tokens)
-    spread = gather(attended, "tp", lines, cross, 2)
-    return combine(spread, out_weight, clean_in, mask_col, mask_embed)
+    return finish(
+        queries, kv_all, kv_noisy, out_weight, clean_in, mask_col, mask_embed, tp, lines, cross
+    )
 
 
 def solution(mesh):

time: 446 us -> 382 us (0.86)
  Pallas kernels: 421 us -> 371 us
  local copies, waits for them, and re-layouts: 19.5 us -> 6.98 us
    pallas_call x2 -> x1, Pallas kernels: 206 us -> 17.3 us  [gather(): pl.pallas_call(functools.partial(gather_kernel, axis, lines, cross), out_...]
    pallas_call x2 -> x1, Pallas kernels: 40.1 us -> 179 us  [finish(): pl.pallas_call(functools.partial(finish_kernel, tp, lines, cross), out_sh...]
    reshape x1 -> x0, local copies, waits for them, and re-layouts: 7.87 us -> none  [per_device(): dealt = jnp.transpose(o_weight.reshape(q_cols, tp, width), (1, 0, 2))]
    unnamed x3 -> x10, local copies, waits for them, and re-layouts: 9.66 us -> 4.69 us
where the time goes in v2:
time: 382 us
  Pallas kernels  371 us (97%)
  local copies, waits for them, and re-layouts  6.98 us (2%)
  other arithmetic  3.89 us (1%)
    pallas_call x1, Pallas kernels, finish(): pl.pallas_call(functools.partial(finish_kernel, tp, lines, cross), out_sh...  179 us
    pallas_call x1, Pallas kernels, first_gather(): pl.pallas_call(functools.partial(first_kernel, tp, seq, lines, cross), ou...  153 us
    pallas_call x1, Pallas kernels, project(): pl.pallas_call(functools.partial(project_kernel, tp), out_shape=(jax.Shap...  21.6 us
    pallas_call x1, Pallas kernels, gather(): pl.pallas_call(functools.partial(gather_kernel, axis, lines, cross), out_...  17.3 us

profile of v2, /device:TPU:0, one launch (start us, length us, event | category | flops | bytes accessed | tf_op | source)
XLA Modules:
  0.0 382.1 jit_solution(9317255635319626525)
XLA Ops:
  0.7 0.5 fusion
  1.2 0.8 pad_maximum_fusion.1
  2.1 0.7 broadcast_in_dim.4
  2.7 2.5 pad_maximum_fusion.own
  5.2 0.0 copy-start.1
  5.2 152.9 %shard_map.113 = (bf16[8,1040,640]{2,1,0:T(8,128)(2,1)}, bf16[4,512,1280]{2,1,0:T(8,128)(2,1)}) custom-call(bf16[1040,640]{1,0:T(8,128)(2,1)} %pad_maximum_fusion.own, bf16[512,5120]{1,0:T(8,128)(2,1)} %weight.1), custom_call_target="tpu_custom_call" | custom-call | tf_op jit(solution)/shard_map/pallas_call | solution.py:207
  158.1 0.0 copy-done.1
  158.1 1.0 copy.15
  159.2 21.6 %shard_map.114 = (bf16[2,1024,512]{2,1,0:T(8,128)(2,1)}, bf16[2,1024,128]{2,1,0:T(8,128)(2,1)}, bf16[2,1024,128]{2,1,0:T(8,128)(2,1)}) custom-call(s32[1]{0:T(128)} %bitcast.head_ref, bf16[8,1040,640]{2,1,0:T(8,128)(2,1)} %get-tuple-element.7.x_ref.m_ref, bf16[8,1040,640]{2,1,0:T(8,128)(2,1)} %get-tuple-element.7.x_ref.m_ref, s32[1024,1]{1,0:T(8,128)} %bitcast.15, ...), custom_call_target="tpu_custom_call" | custom-call | tf_op jit(solution)/shard_map/pallas_call | solution.py:290
  180.8 0.0 copy-start.2
  180.8 17.3 %shard_map.115 = bf16[4,2,1024,128]{3,2,1,0:T(8,128)(2,1)} custom-call(bf16[2,1024,128]{2,1,0:T(8,128)(2,1)} %get-tuple-element.9.own), custom_call_target="tpu_custom_call" | custom-call | tf_op jit(solution)/shard_map/pallas_call | solution.py:136
  198.1 1.0 copy.13.mask_ref
  199.1 0.0 copy-done.2
  199.1 0.6 broadcast_in_dim.5.embed_ref
  199.7 178.8 %shard_map.116 = (bf16[4,256,640]{2,1,0:T(8,128)(2,1)}, bf16[4,256,640]{2,1,0:T(8,128)(2,1)}) custom-call(bf16[2,4,256,512]{3,2,1,0:T(8,128)(2,1)} %bitcast.16, bf16[4,2,4,256,128]{4,3,2,1,0:T(8,128)(2,1)} %bitcast.13, bf16[2,4,256,128]{3,2,1,0:T(8,128)(2,1)} %bitcast.17, bf16[4,512,1280]{2,1,0:T(8,128)(2,1)} %get-tuple-element.11.w_ref, ...), custom_call_target="tpu_custom_call" | custom-call | tf_op jit(solution)/shard_map/pallas_call | solution.py:482
  378.5 0.0 copy-start
  378.5 2.6 copy.18
  381.1 0.0 copy-done
  381.1 1.1 copy.19
  (3 shorter events, 0.0 us)
Async XLA Ops:
  5.2 152.9 %copy-start.1 = (s32[4,256]{1,0:T(4,128)S(1)}, s32[4,256]{1,0:T(4,128)}, u32[]{:S(2)}) copy-start(s32[4,256]{1,0:T(4,128)} %param.11) | copy-start | bytes 12292
  180.8 18.3 %copy-start.2 = (bf16[640]{0:T(1024)(128)(2,1)S(1)}, bf16[640]{0:T(1024)(128)(2,1)}, u32[]{:S(2)}) copy-start(bf16[640]{0:T(1024)(128)(2,1)} %param.12) | copy-start | bytes 3844
  378.5 2.6 copy-start

commit v3 on v2

v3 whole, which is shorter than its diff:
```python
import functools
import math

import jax
import jax.numpy as jnp
from jax import lax
from jax.experimental import pallas as pl
from jax.experimental.pallas import tpu as pltpu
from jax.sharding import PartitionSpec as P

HD = 128
KVH = 8
BLOCK = 32
PAD = 16

eps = 1e-06
theta = 1000000.0
MESH = pl.DeviceIdType.MESH
VMEM_BYTES = 60 * 2**20


def tables(positions):
    half = HD // 2
    freqs = theta ** (-(jnp.arange(half).astype(jnp.float32) * 2.0) / HD)
    angles = positions[:, None] * freqs[None, :]
    cosine = jnp.cos(angles)
    sine = jnp.sin(angles)
    return jnp.concatenate([cosine, cosine], 1), jnp.concatenate([-sine, sine], 1)


def greet(groups):
    barrier = pltpu.get_barrier_semaphore()
    count = 0
    for axis, size in groups:
        me = lax.axis_index(axis)
        for step in range(1, size):
            pl.semaphore_signal(
                barrier, inc=1, device_id={axis: lax.rem(me + step, size)}, device_id_type=MESH
            )
        count += size - 1
    pl.semaphore_wait(barrier, count)


def spin(values, cosine, sine):
    parts = []
    for start in range(0, values.shape[1], HD):
        head = values[:, start : start + HD]
        parts.append(head * cosine + pltpu.roll(head, HD // 2, 1) * sine)
    return jnp.concatenate(parts, 1) if len(parts) > 1 else parts[0]


def first_kernel(
    tp, seq, lines, cross,
    x_ref, embed_ref, mask_ref, gain_ref, qw, qb, kw_any, vw_any, vb, cos_ref, sin_ref, weight,
    q_out, kv_out, kvn_out, wout,
    held, marks, kw, vw, qm, km, vm,
    send, recv, msend, mrecv, kvsend, kvrecv, wsend, wrecv, xsend, xrecv, keep,
):
    greet([("tp", tp), ("seq", seq)])
    me = lax.axis_index("tp")
    s = lax.axis_index("seq")
    a, b = me // cross, lax.rem(me, cross)
    docs, tokens, width = x_ref.shape
    q_cols = qw.shape[1]
    head = pl.ds(pl.multiple_of(me * KVH // tp * HD, HD), HD)
    steps = (cross, tp - cross, 1, tp - 1)
    more = (a + 1 < lines, a > 0, b + 1 < cross, b > 0)

    def pass_on(d, slot, way):
        return pltpu.make_async_remote_copy(
            src_ref=held.at[d, slot],
            dst_ref=held.at[d, slot],
            send_sem=send.at[d, slot, way],
            recv_sem=recv.at[d, slot],
            device_id={"tp": lax.rem(me + steps[way], tp)},
            device_id_type=MESH,
        )

    def mark(e):
        return pltpu.make_async_remote_copy(
            src_ref=marks.at[me],
            dst_ref=marks.at[me],
            send_sem=msend.at[e],
            recv_sem=mrecv.at[e],
            device_id={"tp": lax.rem(me + e, tp)},
            device_id_type=MESH,
        )

    def tell(d, e):
        return pltpu.make_async_remote_copy(
            src_ref=kv_out.at[d, s],
            dst_ref=kv_out.at[d, s],
            send_sem=kvsend.at[d, e],
            recv_sem=kvrecv.at[d, e],
            device_id={"seq": lax.rem(s + e, seq)},
            device_id_type=MESH,
        )

    rows = weight.shape[0] // seq
    cols = weight.shape[1] // lines
    piece = pl.ds(pl.multiple_of(s * rows, rows), rows)

    def deal(e):
        to = lax.rem(a + e, lines)
        return pltpu.make_async_remote_copy(
            src_ref=weight.at[piece, pl.ds(pl.multiple_of(to * cols, 128), cols)],
            dst_ref=wout.at[a, piece],
            send_sem=wsend.at[e],
            recv_sem=wrecv.at[e],
            device_id={"tp": to * cross + b},
            device_id_type=MESH,
        )

    def share(e, f):
        source = lax.rem(a + lines - e, lines)
        return pltpu.make_async_remote_copy(
            src_ref=wout.at[source, piece],
            dst_ref=wout.at[source, piece],
            send_sem=xsend.at[e, f],
            recv_sem=xrecv.at[e, f],
            device_id={"seq": lax.rem(s + f, seq)},
            device_id_type=MESH,
        )

    stays = (
        pltpu.make_async_copy(
            weight.at[:, pl.ds(pl.multiple_of(a * cols, 128), cols)], wout.at[a], keep.at[0]
        ),
        pltpu.make_async_copy(kw_any.at[:, head], kw, keep.at[1]),
        pltpu.make_async_copy(vw_any.at[:, head], vw, keep.at[2]),
    )
    marks[me] = jnp.broadcast_to(embed_ref[...], (PAD, width))
    for e in range(1, tp):
        mark(e).start()
    for copy in stays:
        copy.start()

    def places(r):
        return ((0, a - r >= 0, a - r), (1, a + r < lines, a + r))

    def along(r, d):
        for way, here, line in places(r):
            slot = line * cross + b

            @pl.when(here)
            def _():
                pass_on(d, slot, way).wait_recv()

            for out in (way, 2, 3):

                @pl.when(jnp.logical_and(here, more[out]))
                def _():
                    pass_on(d, slot, out).start()

    def columns(r):
        return ((2, b - r >= 0, b - r), (3, b + r < cross, b + r))

    def across(d):
        for r in range(1, cross):
            for way, here, col in columns(r):
                for line in range(lines):

                    @pl.when(here)
                    def _():
                        pass_on(d, line * cross + col, way).wait_recv()

                    if cross > 2:

                        @pl.when(jnp.logical_and(here, more[way]))
                        def _():
                            pass_on(d, line * cross + col, way).start()

    def project(part_of):
        rows = part_of(0).shape[0]
        total = jnp.zeros((rows, 1), jnp.float32)
        for t in range(tp):
            part = part_of(t).astype(jnp.float32)
            total = total + jnp.sum(part * part, axis=1, keepdims=True)
        scale = lax.rsqrt(total / (tp * width) + eps)
        q = jnp.zeros((rows, q_cols), jnp.float32)
        k = jnp.zeros((rows, HD), jnp.float32)
        v = jnp.zeros((rows, HD), jnp.float32)
        for t in range(tp):
            here = pl.ds(t * width, width)
            normed = (part_of(t).astype(jnp.float32) * scale * gain_ref[t]).astype(jnp.bfloat16)
            q = q + jnp.dot(normed, qw[here, :], preferred_element_type=jnp.float32)
            k = k + jnp.dot(normed, kw[here, :], preferred_element_type=jnp.float32)
            v = v + jnp.dot(normed, vw[here, :], preferred_element_type=jnp.float32)
        return q + qb[...], k, v + vb[me * KVH // tp]

    def wave(step, carry):
        @pl.when(step < docs)
        def _():
            held[step, me] = x_ref[step]
            for way in range(4):

                @pl.when(more[way])
                def _():
                    pass_on(step, me, way).start()

        @pl.when(step == 1)
        def _():
            for e in range(1, lines):
                deal(e).start()

        for r in range(1, lines):

            @pl.when(jnp.logical_and(step >= r, step < docs + r))
            def _():
                along(r, step - r)

        @pl.when(step == lines)
        def _():
            for e in range(1, tp):
                mark(e).wait_recv()
            stays[1].wait()
            stays[2].wait()
            qm[...], km[...], vm[...] = project(lambda t: marks[t])

        @pl.when(step >= lines)
        def _():
            d = step - lines
            across(d)
            cosine, sine = cos_ref[...], sin_ref[...]
            q, k, v = project(lambda t: held[d, t])
            q = spin(q, cosine, sine)
            k = spin(k, cosine, sine)
            kv_out[d, s, 0] = k.astype(jnp.bfloat16)
            kv_out[d, s, 1] = v.astype(jnp.bfloat16)
            for e in range(1, seq):
                tell(d, e).start()
            masked = mask_ref[d] == 1
            q_mask = spin(jnp.broadcast_to(qm[0:1, :], (tokens, q_cols)), cosine, sine)
            k_mask = spin(jnp.broadcast_to(km[0:1, :], (tokens, HD)), cosine, sine)
            v_mask = jnp.broadcast_to(vm[0:1, :], (tokens, HD))
            q_out[0, d] = q.astype(jnp.bfloat16)
            q_out[1, d] = jnp.where(masked, q_mask, q).astype(jnp.bfloat16)
            kvn_out[0, d] = jnp.where(masked, k_mask, k).astype(jnp.bfloat16)
            kvn_out[1, d] = jnp.where(masked, v_mask, v).astype(jnp.bfloat16)

        @pl.when(step == lines)
        def _():
            for e in range(1, lines):
                deal(e).wait_recv()
                for f in range(1, seq):
                    share(e, f).start()

        return carry

    lax.fori_loop(0, docs + lines, wave, 0)

    def close(d, carry):
        for e in range(1, seq):
            tell(d, e).wait()
        for r in range(lines):
            for way, here, line in places(r):
                slot = line * cross + b
                outs = (way, way + 2) if r == 0 else (way, 2, 3)
                for out in outs:

                    @pl.when(jnp.logical_and(here, more[out]))
                    def _():
                        pass_on(d, slot, out).wait_send()

        if cross > 2:
            for r in range(1, cross):
                for way, here, col in columns(r):
                    for line in range(lines):

                        @pl.when(jnp.logical_and(here, more[way]))
                        def _():
                            pass_on(d, line * cross + col, way).wait_send()

        return carry

    lax.fori_loop(0, docs, close, 0)
    for e in range(1, tp):
        mark(e).wait_send()
    for e in range(1, lines):
        deal(e).wait_send()
        for f in range(1, seq):
            share(e, f).wait()
    stays[0].wait()


def first(
    clean_in, mask_col, mask_embed, gain, q_weight, q_bias, k_weight, v_weight, v_bias,
    cosine, sine, weight, tp, seq, lines, cross,
):
    docs, tokens, width = clean_in.shape
    d_model, q_cols = q_weight.shape
    vmem = pl.BlockSpec(memory_space=pltpu.VMEM)
    anywhere = pl.BlockSpec(memory_space=pl.ANY)
    dma = pltpu.SemaphoreType.DMA
    bf16 = jnp.bfloat16
    return pl.pallas_call(
        functools.partial(first_kernel, tp, seq, lines, cross),
        out_shape=(
            jax.ShapeDtypeStruct((2, docs, tokens, q_cols), bf16),
            jax.ShapeDtypeStruct((docs, seq, 2, tokens, HD), bf16),
            jax.ShapeDtypeStruct((2, docs, tokens, HD), bf16),
            jax.ShapeDtypeStruct((lines, q_cols, d_model // lines), bf16),
        ),
        in_specs=[vmem] * 6 + [anywhere] * 2 + [vmem] * 3 + [anywhere],
        out_specs=(vmem, vmem, vmem, anywhere),
        scratch_shapes=[
            pltpu.VMEM((docs, tp, tokens, width), bf16),
            pltpu.VMEM((tp, PAD, width), bf16),
            pltpu.VMEM((d_model, HD), bf16),
            pltpu.VMEM((d_model, HD), bf16),
            pltpu.VMEM((PAD, q_cols), jnp.float32),
            pltpu.VMEM((PAD, HD), jnp.float32),
            pltpu.VMEM((PAD, HD), jnp.float32),
            dma((docs, tp, 4)),
            dma((docs, tp)),
            dma((tp,)),
            dma((tp,)),
            dma((docs, seq)),
            dma((docs, seq)),
            dma((lines,)),
            dma((lines,)),
            dma((lines, seq)),
            dma((lines, seq)),
            dma((3,)),
        ],
        compiler_params=pltpu.CompilerParams(
            collective_id=0, has_side_effects=True, vmem_limit_bytes=VMEM_BYTES
        ),
    )(
        clean_in, mask_embed.reshape(1, width), mask_col, gain.reshape(tp, 1, width), q_weight,
        q_bias.reshape(1, -1), k_weight, v_weight, v_bias.reshape(-1, 1, HD), cosine, sine, weight,
    )


def finish_kernel(
    tp, lines, cross, q_ref, kv_ref, kvn_ref, w_ref, x_ref, mask_ref, embed_ref, clean_ref, noisy_ref,
    heads_ref, total_ref, leave_ref, come_ref, send, recv, psend, precv,
):
    greet([("tp", tp)])
    me = lax.axis_index("tp")
    a, b = me // cross, lax.rem(me, cross)
    docs, seq, _, tokens, _ = kv_ref.shape
    q_cols = q_ref.shape[3]
    width = x_ref.shape[2]
    keys = seq * tokens
    scale = 1.0 / math.sqrt(HD)

    def blocks(count, axis, start):
        return (start + lax.broadcasted_iota(jnp.int32, (tokens, count), axis)) // BLOCK

    q_block = blocks(keys, 0, lax.axis_index("seq") * tokens)
    k_block = blocks(keys, 1, 0)
    clean_bias = jnp.where(k_block <= q_block, 0.0, -1e30)
    noisy_bias = jnp.where(k_block < q_block, 0.0, -1e30)
    own_bias = jnp.where(blocks(tokens, 1, 0) == blocks(tokens, 0, 0), 0.0, -1e30)

    def scores(q, k, bias):
        dims = (((1,), (1,)), ((), ()))
        return lax.dot_general(q, k, dims, preferred_element_type=jnp.float32) * scale + bias

    def weigh(expo, v):
        return jnp.dot(expo.astype(jnp.bfloat16), v, preferred_element_type=jnp.float32)

    def pass_on(d, slot, way):
        return pltpu.make_async_remote_copy(
            src_ref=heads_ref.at[d, slot],
            dst_ref=heads_ref.at[d, slot],
            send_sem=send.at[d, slot, way],
            recv_sem=recv.at[d, slot],
            device_id={"tp": lax.rem(me + (cross, tp - cross)[way], tp)},
            device_id_type=MESH,
        )

    more = (a + 1 < lines, a > 0)

    def attend(d):
        k_all = kv_ref[d, :, 0].reshape(keys, HD)
        v_all = kv_ref[d, :, 1].reshape(keys, HD)
        k_own, v_own = kvn_ref[0, d], kvn_ref[1, d]
        for h in range(q_cols // HD):
            cols = pl.ds(h * HD, HD)
            s = scores(q_ref[0, d, :, cols], k_all, clean_bias)
            expo = jnp.exp(s - jnp.max(s, axis=1, keepdims=True))
            denom = jnp.sum(expo, axis=1, keepdims=True)
            heads_ref[d, a, 0, :, cols] = (weigh(expo, v_all) / denom).astype(jnp.bfloat16)
            q = q_ref[1, d, :, cols]
            s = scores(q, k_all, noisy_bias)
            t = scores(q, k_own, own_bias)
            best = jnp.maximum(jnp.max(s, axis=1, keepdims=True), jnp.max(t, axis=1, keepdims=True))
            expo_s, expo_t = jnp.exp(s - best), jnp.exp(t - best)
            denom = jnp.sum(expo_s, axis=1, keepdims=True) + jnp.sum(expo_t, axis=1, keepdims=True)
            total = weigh(expo_s, v_all) + weigh(expo_t, v_own)
            heads_ref[d, a, 1, :, cols] = (total / denom).astype(jnp.bfloat16)
        for way in range(2):

            @pl.when(more[way])
            def _():
                pass_on(d, a, way).start()

    def along(r, d):
        for way, here, slot in ((0, a - r >= 0, a - r), (1, a + r < lines, a + r)):

            @pl.when(here)
            def _():
                pass_on(d, slot, way).wait_recv()

            @pl.when(jnp.logical_and(here, more[way]))
            def _():
                pass_on(d, slot, way).start()

    def partial(d, e):
        return pltpu.make_async_remote_copy(
            src_ref=leave_ref.at[d, e],
            dst_ref=come_ref.at[d, e],
            send_sem=psend.at[d, e],
            recv_sem=precv.at[d, e],
            device_id={"tp": a * cross + lax.rem(b + e, cross)},
            device_id_type=MESH,
        )

    def multiply(d):
        for stream in range(2):
            total = jnp.zeros((tokens, cross * width), jnp.float32)
            for line in range(lines):
                total = total + jnp.dot(
                    heads_ref[d, line, stream], w_ref[line], preferred_element_type=jnp.float32
                )
            for target in range(cross):
                part = total[:, target * width : (target + 1) * width]

                @pl.when(b == target)
                def _():
                    total_ref[d, stream] = part

                @pl.when(b != target)
                def _():
                    leave_ref[d, lax.rem(target - b + cross, cross), stream] = part.astype(
                        jnp.bfloat16
                    )

        for e in range(1, cross):
            partial(d, e).start()

    def wave(step, carry):
        @pl.when(step < docs)
        def _():
            attend(step)

        for r in range(1, lines):

            @pl.when(jnp.logical_and(step >= r, step < docs + r))
            def _():
                along(r, step - r)

        @pl.when(step >= lines - 1)
        def _():
            multiply(step - (lines - 1))

        return carry

    lax.fori_loop(0, docs + lines - 1, wave, 0)

    def close(d, carry):
        clean = x_ref[d].astype(jnp.float32)
        noisy = jnp.where(mask_ref[d] == 1, embed_ref[...].astype(jnp.float32), clean)
        for e in range(1, cross):
            partial(d, e).wait_recv()
        for stream, base, out in ((0, clean, clean_ref), (1, noisy, noisy_ref)):
            total = total_ref[d, stream]
            for e in range(1, cross):
                total = total + come_ref[d, e, stream].astype(jnp.float32)
            out[d] = (base + total).astype(jnp.bfloat16)
        for e in range(1, cross):
            partial(d, e).wait_send()
        for r in range(lines):
            for way, here, slot in ((0, a - r >= 0, a - r), (1, a + r < lines, a + r)):

                @pl.when(jnp.logical_and(here, more[way]))
                def _():
                    pass_on(d, slot, way).wait_send()

        return carry

    lax.fori_loop(0, docs, close, 0)


def finish(queries, kv_all, kv_noisy, weight, clean_in, mask_col, mask_embed, tp, lines, cross):
    docs, tokens, width = clean_in.shape
    q_cols = queries.shape[3]
    out = jax.ShapeDtypeStruct(clean_in.shape, jnp.bfloat16)
    vmem = pl.BlockSpec(memory_space=pltpu.VMEM)
    dma = pltpu.SemaphoreType.DMA
    return pl.pallas_call(
        functools.partial(finish_kernel, tp, lines, cross),
        out_shape=(out, out),
        in_specs=[vmem] * 7,
        out_specs=(vmem, vmem),
        scratch_shapes=[
            pltpu.VMEM((docs, lines, 2, tokens, q_cols), jnp.bfloat16),
            pltpu.VMEM((docs, 2, tokens, width), jnp.float32),
            pltpu.VMEM((docs, cross, 2, tokens, width), jnp.bfloat16),
            pltpu.VMEM((docs, cross, 2, tokens, width), jnp.bfloat16),
            dma((docs, lines, 2)),
            dma((docs, lines)),
            dma((docs, cross)),
            dma((docs, cross)),
        ],
        compiler_params=pltpu.CompilerParams(
            collective_id=2, has_side_effects=True, vmem_limit_bytes=VMEM_BYTES
        ),
    )(
        queries,
        kv_all,
        kv_noisy,
        weight,
        clean_in,
        mask_col,
        mask_embed.reshape(1, width),
    )


def per_device(
    tp,
    seq,
    clean_in,
    noise_mask,
    mask_embed,
    norm_gain,
    q_weight,
    q_bias,
    k_weight,
    v_weight,
    v_bias,
    o_weight,
):
    docs, tokens, _ = clean_in.shape
    lines = 4 if tp % 4 == 0 else 1
    cross = tp // lines
    my_seq = lax.axis_index("seq")
    mask_col = noise_mask.reshape(docs, tokens, 1)
    positions = (my_seq * tokens + jnp.arange(tokens)).astype(jnp.float32)
    cosine, sine = tables(positions)
    queries, kv_all, kv_noisy, out_weight = first(
        clean_in, mask_col, mask_embed, norm_gain, q_weight, q_bias, k_weight, v_weight, v_bias,
        cosine, sine, o_weight, tp, seq, lines, cross,
    )
    return finish(
        queries, kv_all, kv_noisy, out_weight, clean_in, mask_col, mask_embed, tp, lines, cross
    )


def solution(mesh):
    return jax.shard_map(
        functools.partial(per_device, mesh.shape["tp"], mesh.shape["seq"]),
        mesh=mesh,
        in_specs=(
            P(None, "seq", "tp"),
            P(None, "seq"),
            P("tp"),
            P(),
            P(None, "tp"),
            P("tp"),
            P(),
            P(),
            P(),
            P("tp", None),
        ),
        out_specs=(P(None, "seq", "tp"), P(None, "seq", "tp")),
        check_vma=False,
    )
```

time: 382 us -> 355 us (0.929)
  Pallas kernels: 371 us -> 346 us
    pallas_call x3 -> x1, Pallas kernels: 192 us -> 172 us  [first(): pl.pallas_call(functools.partial(first_kernel, tp, seq, lines, cross), ou...]
    pallas_call x1, Pallas kernels: 179 us -> 174 us  [finish(): pl.pallas_call(functools.partial(finish_kernel, tp, lines, cross), out_sh...]
where the time goes in v3:
time: 355 us
  Pallas kernels  346 us (97%)
  local copies, waits for them, and re-layouts  6.6 us (2%)
    pallas_call x1, Pallas kernels, finish(): pl.pallas_call(functools.partial(finish_kernel, tp, lines, cross), out_sh...  174 us
    pallas_call x1, Pallas kernels, first(): pl.pallas_call(functools.partial(first_kernel, tp, seq, lines, cross), ou...  172 us

profile of v3, /device:TPU:0, one launch (start us, length us, event | category | flops | bytes accessed | tf_op | source)
XLA Modules:
  0.0 354.9 jit_solution(5232198150153907869)
XLA Ops:
  0.7 1.3 reshape.33.embed_ref
  1.9 0.5 fusion
  2.4 0.8 pad_maximum_fusion
  3.3 1.7 copy.12.mask_ref
  5.0 171.8 %shard_map.113 = (bf16[2,4,256,512]{3,2,1,0:T(8,128)(2,1)}, bf16[4,4,2,256,128]{4,3,2,1,0:T(8,128)(2,1)}, bf16[2,4,256,128]{3,2,1,0:T(8,128)(2,1)}, bf16[4,512,1280]{2,1,0:T(8,128)(2,1)}) custom-call(bf16[4,256,640]{2,1,0:T(8,128)(2,1)} %x_ref.3, bf16[1,640]{1,0:T(2,128)(2,1)} %reshape.33.embed_ref, s32[4,256,1]{2,1,0:T(8,128)} %copy.12.mask_ref, ...), custom_call_target="tpu_custom_call" | custom-call | tf_op jit(solution)/shard_map/pallas_call | solution.py:296
  176.8 174.5 %shard_map.114 = (bf16[4,256,640]{2,1,0:T(8,128)(2,1)}, bf16[4,256,640]{2,1,0:T(8,128)(2,1)}) custom-call(bf16[2,4,256,512]{3,2,1,0:T(8,128)(2,1)} %get-tuple-element.6.q_ref, bf16[4,4,2,256,128]{4,3,2,1,0:T(8,128)(2,1)} %get-tuple-element.7.kv_ref, bf16[2,4,256,128]{3,2,1,0:T(8,128)(2,1)} %get-tuple-element.8.kvn_ref, ...), custom_call_target="tpu_custom_call" | custom-call | tf_op jit(solution)/shard_map/pallas_call | solution.py:493
  351.2 0.0 copy-start
  351.3 2.6 copy.16
  353.8 0.0 copy-done
  353.8 1.1 copy.17
  (2 shorter events, 0.0 us)
Async XLA Ops:
  351.2 2.6 copy-start

commit v4 on v3

--- a/solution.py
+++ b/solution.py
@@ -188,15 +188,17 @@
             v = v + jnp.dot(normed, vw[here, :], preferred_element_type=jnp.float32)
         return q + qb[...], k, v + vb[me * KVH // tp]
 
+    last = docs + lines - 2
+
     def wave(step, carry):
-        @pl.when(step < docs)
-        def _():
-            held[step, me] = x_ref[step]
+        @pl.when(step + 1 < docs)
+        def _():
+            held[step + 1, me] = x_ref[step + 1]
             for way in range(4):
 
                 @pl.when(more[way])
                 def _():
-                    pass_on(step, me, way).start()
+                    pass_on(step + 1, me, way).start()
 
         @pl.when(step == 1)
         def _():
@@ -209,7 +211,7 @@
             def _():
                 along(r, step - r)
 
-        @pl.when(step == lines)
+        @pl.when(step == last)
         def _():
             for e in range(1, tp):
                 mark(e).wait_recv()
@@ -217,9 +219,9 @@
             stays[2].wait()
             qm[...], km[...], vm[...] = project(lambda t: marks[t])
 
-        @pl.when(step >= lines)
-        def _():
-            d = step - lines
+        @pl.when(step >= last)
+        def _():
+            d = step - last
             across(d)
             cosine, sine = cos_ref[...], sin_ref[...]
             q, k, v = project(lambda t: held[d, t])
@@ -247,7 +249,7 @@
 
         return carry
 
-    lax.fori_loop(0, docs + lines, wave, 0)
+    lax.fori_loop(-1, last + docs, wave, 0)
 
     def close(d, carry):
         for e in range(1, seq):
@@ -442,9 +444,9 @@
             partial(d, e).start()
 
     def wave(step, carry):
-        @pl.when(step < docs)
-        def _():
-            attend(step)
+        @pl.when(step + 1 < docs)
+        def _():
+            attend(step + 1)
 
         for r in range(1, lines):
 
@@ -458,7 +460,7 @@
 
         return carry
 
-    lax.fori_loop(0, docs + lines - 1, wave, 0)
+    lax.fori_loop(-1, docs + lines - 1, wave, 0)
 
     def close(d, carry):
         clean = x_ref[d].astype(jnp.float32)

time: 355 us -> 350 us (0.986)
  Pallas kernels: 346 us -> 341 us
    pallas_call x1, Pallas kernels: 172 us -> 167 us  [first(): pl.pallas_call(functools.partial(first_kernel, tp, seq, lines, cross), ou...]
where the time goes in v4:
time: 350 us
  Pallas kernels  341 us (97%)
  local copies, waits for them, and re-layouts  6.6 us (2%)
    pallas_call x1, Pallas kernels, finish(): pl.pallas_call(functools.partial(finish_kernel, tp, lines, cross), out_sh...  174 us
    pallas_call x1, Pallas kernels, first(): pl.pallas_call(functools.partial(first_kernel, tp, seq, lines, cross), ou...  167 us

profile of v4, /device:TPU:0, one launch (start us, length us, event | category | flops | bytes accessed | tf_op | source)
XLA Modules:
  0.0 350.0 jit_solution(3019904500698787142)
XLA Ops:
  0.7 1.3 reshape.33.embed_ref
  1.9 0.5 fusion
  2.4 0.8 pad_maximum_fusion
  3.3 1.7 copy.12.mask_ref
  5.0 166.9 %shard_map.113 = (bf16[2,4,256,512]{3,2,1,0:T(8,128)(2,1)}, bf16[4,4,2,256,128]{4,3,2,1,0:T(8,128)(2,1)}, bf16[2,4,256,128]{3,2,1,0:T(8,128)(2,1)}, bf16[4,512,1280]{2,1,0:T(8,128)(2,1)}) custom-call(bf16[4,256,640]{2,1,0:T(8,128)(2,1)} %x_ref.3, bf16[1,640]{1,0:T(2,128)(2,1)} %reshape.33.embed_ref, s32[4,256,1]{2,1,0:T(8,128)} %copy.12.mask_ref, ...), custom_call_target="tpu_custom_call" | custom-call | tf_op jit(solution)/shard_map/pallas_call | solution.py:298
  171.9 174.5 %shard_map.114 = (bf16[4,256,640]{2,1,0:T(8,128)(2,1)}, bf16[4,256,640]{2,1,0:T(8,128)(2,1)}) custom-call(bf16[2,4,256,512]{3,2,1,0:T(8,128)(2,1)} %get-tuple-element.6.q_ref, bf16[4,4,2,256,128]{4,3,2,1,0:T(8,128)(2,1)} %get-tuple-element.7.kv_ref, bf16[2,4,256,128]{3,2,1,0:T(8,128)(2,1)} %get-tuple-element.8.kvn_ref, ...), custom_call_target="tpu_custom_call" | custom-call | tf_op jit(solution)/shard_map/pallas_call | solution.py:495
  346.4 0.0 copy-start
  346.4 2.6 copy.16
  349.0 0.0 copy-done
  349.0 1.1 copy.17
  (2 shorter events, 0.0 us)
Async XLA Ops:
  346.4 2.6 copy-start

commit v5 on v4

--- a/solution.py
+++ b/solution.py
@@ -53,7 +53,7 @@
     tp, seq, lines, cross,
     x_ref, embed_ref, mask_ref, gain_ref, qw, qb, kw_any, vw_any, vb, cos_ref, sin_ref, weight,
     q_out, kv_out, kvn_out, wout,
-    held, marks, kw, vw, qm, km, vm,
+    held, marks, kvw, qm, km, vm,
     send, recv, msend, mrecv, kvsend, kvrecv, wsend, wrecv, xsend, xrecv, keep,
 ):
     greet([("tp", tp), ("seq", seq)])
@@ -126,8 +126,8 @@
         pltpu.make_async_copy(
             weight.at[:, pl.ds(pl.multiple_of(a * cols, 128), cols)], wout.at[a], keep.at[0]
         ),
-        pltpu.make_async_copy(kw_any.at[:, head], kw, keep.at[1]),
-        pltpu.make_async_copy(vw_any.at[:, head], vw, keep.at[2]),
+        pltpu.make_async_copy(kw_any.at[:, head], kvw.at[:, pl.ds(0, HD)], keep.at[1]),
+        pltpu.make_async_copy(vw_any.at[:, head], kvw.at[:, pl.ds(HD, HD)], keep.at[2]),
     )
     marks[me] = jnp.broadcast_to(embed_ref[...], (PAD, width))
     for e in range(1, tp):
@@ -178,15 +178,13 @@
             total = total + jnp.sum(part * part, axis=1, keepdims=True)
         scale = lax.rsqrt(total / (tp * width) + eps)
         q = jnp.zeros((rows, q_cols), jnp.float32)
-        k = jnp.zeros((rows, HD), jnp.float32)
-        v = jnp.zeros((rows, HD), jnp.float32)
+        kv = jnp.zeros((rows, 2 * HD), jnp.float32)
         for t in range(tp):
             here = pl.ds(t * width, width)
             normed = (part_of(t).astype(jnp.float32) * scale * gain_ref[t]).astype(jnp.bfloat16)
             q = q + jnp.dot(normed, qw[here, :], preferred_element_type=jnp.float32)
-            k = k + jnp.dot(normed, kw[here, :], preferred_element_type=jnp.float32)
-            v = v + jnp.dot(normed, vw[here, :], preferred_element_type=jnp.float32)
-        return q + qb[...], k, v + vb[me * KVH // tp]
+            kv = kv + jnp.dot(normed, kvw[here, :], preferred_element_type=jnp.float32)
+        return q + qb[...], kv[:, :HD], kv[:, HD:] + vb[me * KVH // tp]
 
     last = docs + lines - 2
 
@@ -211,7 +209,7 @@
             def _():
                 along(r, step - r)
 
-        @pl.when(step == last)
+        @pl.when(step == 1)
         def _():
             for e in range(1, tp):
                 mark(e).wait_recv()
@@ -308,8 +306,7 @@
         scratch_shapes=[
             pltpu.VMEM((docs, tp, tokens, width), bf16),
             pltpu.VMEM((tp, PAD, width), bf16),
-            pltpu.VMEM((d_model, HD), bf16),
-            pltpu.VMEM((d_model, HD), bf16),
+            pltpu.VMEM((d_model, 2 * HD), bf16),
             pltpu.VMEM((PAD, q_cols), jnp.float32),
             pltpu.VMEM((PAD, HD), jnp.float32),
             pltpu.VMEM((PAD, HD), jnp.float32),

time: 350 us -> 350 us (level)
  no operation moved by 1% of the time
where the time goes in v5:
time: 350 us
  Pallas kernels  341 us (97%)
  local copies, waits for them, and re-layouts  6.6 us (2%)
    pallas_call x1, Pallas kernels, finish(): pl.pallas_call(functools.partial(finish_kernel, tp, lines, cross), out_sh...  174 us
    pallas_call x1, Pallas kernels, first(): pl.pallas_call(functools.partial(first_kernel, tp, seq, lines, cross), ou...  167 us

profile of v5, /device:TPU:0, one launch (start us, length us, event | category | flops | bytes accessed | tf_op | source)
XLA Modules:
  0.0 350.0 jit_solution(1519486400586566156)
XLA Ops:
  0.7 1.3 reshape.33.embed_ref
  1.9 0.5 fusion
  2.4 0.8 pad_maximum_fusion
  3.3 1.7 copy.12.mask_ref
  5.0 166.9 %shard_map.113 = (bf16[2,4,256,512]{3,2,1,0:T(8,128)(2,1)}, bf16[4,4,2,256,128]{4,3,2,1,0:T(8,128)(2,1)}, bf16[2,4,256,128]{3,2,1,0:T(8,128)(2,1)}, bf16[4,512,1280]{2,1,0:T(8,128)(2,1)}) custom-call(bf16[4,256,640]{2,1,0:T(8,128)(2,1)} %x_ref.3, bf16[1,640]{1,0:T(2,128)(2,1)} %reshape.33.embed_ref, s32[4,256,1]{2,1,0:T(8,128)} %copy.12.mask_ref, ...), custom_call_target="tpu_custom_call" | custom-call | tf_op jit(solution)/shard_map/pallas_call | solution.py:296
  171.9 174.5 %shard_map.114 = (bf16[4,256,640]{2,1,0:T(8,128)(2,1)}, bf16[4,256,640]{2,1,0:T(8,128)(2,1)}) custom-call(bf16[2,4,256,512]{3,2,1,0:T(8,128)(2,1)} %get-tuple-element.6.q_ref, bf16[4,4,2,256,128]{4,3,2,1,0:T(8,128)(2,1)} %get-tuple-element.7.kv_ref, bf16[2,4,256,128]{3,2,1,0:T(8,128)(2,1)} %get-tuple-element.8.kvn_ref, ...), custom_call_target="tpu_custom_call" | custom-call | tf_op jit(solution)/shard_map/pallas_call | solution.py:492
  346.4 0.0 copy-start
  346.4 2.6 copy.16
  349.0 0.0 copy-done
  349.0 1.1 copy.17
  (2 shorter events, 0.0 us)
Async XLA Ops:
  346.4 2.6 copy-start
